TPU v7x, 256 devices: a whole 4x4x8 slice. The times are simulated.
256 devices in a mesh: ctx: 64 (over z, x_hi, y), head: 4 (over x_lo, core).
Axes of the slice: x: 4 (x_hi: 2, x_lo: 2; x = x_hi * 2 + x_lo), y: 4, z: 8, core: 2. Of those that a mesh axis runs over, the one named last changes fastest.
Arguments:
- ctx_query: bfloat16 [32768, 8192], P('ctx', 'head'), may hold values from -300 to 300
- ctx_key: bfloat16 [32768, 1024], P('ctx', 'head'), may hold values from -10 to 10
- ctx_value: bfloat16 [32768, 1024], P('ctx', 'head'), may hold values from -6 to 6
- valid: int32 [64], P('ctx'), may hold values from 1 to 512, as said below
- query_rows: bfloat16 [256, 8192], P(('ctx', 'head')), may hold values from -300 to 300
- offsets: int32 [256], P(('ctx', 'head')), may hold values from 512 to 32768, as said below
Outputs:
- block_out: bfloat16 [32768, 8192], P('ctx', 'head')
- query_out: bfloat16 [256, 8192], P(('ctx', 'head'))
Inputs may be any that keep to these rules, and one draw needn't show every extreme that they name: Every block but the last holds 512 valid tokens. `offsets`: some row sees all 32768 context positions and some row only the first block.
All inputs are finite; a program needn't handle non-finite values.
Results may differ from a plain program's by a relative error of at most 0.0045.
Values may be sent and summed in bfloat16 or wider, within the bound.
No kernel may reach another device: no remote copies, remote signals or barrier semaphores. Data moves between devices by JAX's collectives and lax.ppermute only.
A program may use at most 64 MiB of HBM per device.

v0:
```python
import math

import jax
import jax.numpy as jnp
from jax import lax
from jax.sharding import PartitionSpec as P

QHEADS = 64
KVHEADS = 8
DH = 128


def broadcast(value, axis, source):
    kept = jnp.where(lax.axis_index(axis) == source, value, 0).astype(value.dtype)
    return lax.psum(kept, axis)


def head_terms(queries, key_block, value_block, visible):
    scores = jnp.einsum("qd,kd->qk", queries, key_block, preferred_element_type=jnp.float32) * (
        1.0 / math.sqrt(DH)
    )
    highest = jnp.max(jnp.where(visible, scores, -1e30), axis=1)
    weights = jnp.where(visible, jnp.exp(scores - highest[:, None]), 0.0)
    totals = jnp.sum(weights, axis=1)
    summed = jnp.dot(weights.astype(jnp.bfloat16), value_block, preferred_element_type=jnp.float32)
    return (highest, totals, summed)


def head_columns(array, head_index):
    return lax.dynamic_slice_in_dim(array, head_index * DH, DH, 1)


def on_device(ctx_query, ctx_key, ctx_value, valid, query_rows, offsets):
    group_size = QHEADS // KVHEADS
    length = ctx_query.shape[0]
    heads_here = ctx_query.shape[1] // DH
    block_index = lax.axis_index("ctx")
    row_ids = jnp.arange(length, dtype=jnp.int32)
    anchor_pair = broadcast(jnp.stack([ctx_key, ctx_value]), "ctx", 0)
    key_rows = jnp.concatenate([anchor_pair[0], ctx_key], axis=0)
    value_rows = jnp.concatenate([anchor_pair[1], ctx_value], axis=0)
    own_keys = (row_ids[None, :] <= row_ids[:, None]) & (row_ids[None, :] < valid[0])
    anchor_seen = jnp.broadcast_to(block_index > 0, (length, length))
    visible = jnp.concatenate([anchor_seen, own_keys], axis=1)

    def phase_one(head_index):
        kv_index = head_index // group_size
        highest, totals, summed = head_terms(
            head_columns(ctx_query, head_index),
            head_columns(key_rows, kv_index),
            head_columns(value_rows, kv_index),
            visible,
        )
        return (summed / totals[:, None]).astype(jnp.bfloat16)

    head_outputs = lax.map(phase_one, jnp.arange(heads_here, dtype=jnp.int32))
    block_out = jnp.transpose(head_outputs, (1, 0, 2)).reshape(length, heads_here * DH)
    everything = lax.all_gather(query_rows, ("ctx", "head"), axis=0, tiled=True)
    queries = lax.dynamic_slice_in_dim(
        everything, lax.axis_index("head") * heads_here * DH, heads_here * DH, 1
    )
    offsets_all = lax.all_gather(offsets, ("ctx", "head"), axis=0, tiled=True)
    positions = block_index * length + row_ids
    reachable = (row_ids[None, :] < valid[0]) & (positions[None, :] < offsets_all[:, None])

    def phase_two(head_index):
        kv_index = head_index // group_size
        return head_terms(
            head_columns(queries, head_index),
            head_columns(ctx_key, kv_index),
            head_columns(ctx_value, kv_index),
            reachable,
        )

    highest, totals, summed = lax.map(phase_two, jnp.arange(heads_here, dtype=jnp.int32))
    highest = jnp.transpose(highest)
    totals = jnp.transpose(totals)
    summed = jnp.transpose(summed, (1, 0, 2))
    row_count = queries.shape[0]
    ctx_count = lax.axis_size("ctx")
    owned = row_count // ctx_count
    overall = lax.pmax(highest, "ctx")
    factor = jnp.exp(highest - overall)
    scaled_sums = (summed * factor[..., None]).reshape(row_count, heads_here * DH)
    numerator, denominator = (
        lax.psum_scatter(scaled_sums, "ctx", scatter_dimension=0, tiled=True),
        lax.psum_scatter(totals * factor, "ctx", scatter_dimension=0, tiled=True),
    )
    numerator = numerator.reshape(owned, heads_here, DH)
    merged_rows = (
        (numerator / denominator[..., None]).reshape(owned, heads_here * DH).astype(jnp.bfloat16)
    )
    query_out = lax.all_to_all(merged_rows, "head", split_axis=0, concat_axis=1, tiled=True)
    return (block_out, query_out)


def solution(mesh):
    return jax.shard_map(
        on_device,
        mesh=mesh,
        in_specs=(
            P("ctx", "head"),
            P("ctx", "head"),
            P("ctx", "head"),
            P("ctx"),
            P(("ctx", "head"), None),
            P(("ctx", "head")),
        ),
        out_specs=(P("ctx", "head"), P(("ctx", "head"), None)),
        check_vma=False,
    )
```

profile of v0, /device:TPU:1, one launch (start us, length us, event | category | flops | bytes accessed | tf_op | source)
XLA Modules:
  0.0 1906.5 jit_solution(8200414204719388181)
XLA Ops:
  8.1 2.0 maximum_select_fusion
  13.9 82.2 %all-reduce.1 = s32[256]{0:T(256)S(1)} all-reduce(s32[256]{0:T(256)S(1)} %dynamic-update-slice), channel_id=1, replica_groups=mesh['ctx'=64,'head'=4] {'ctx','head'}, use_global_device_ids=true, to_apply=%add.1 | all-reduce | flops 256 | bytes 2048
  96.1 568.2 %all-reduce.7.cloned.1.call-done = bf16[2,512,256]{2,1,0:T(8,128)(2,1)} async-done(((bf16[2,512,256]{2,1,0:T(8,128)(2,1)}), bf16[2,512,256]{2,1,0:T(8,128)(2,1)}) %all-reduce.7.cloned.1.call-update) | async-done | bytes 524304 | tf_op jit(solution)/shard_map/psum | solution.py:15
  665.3 1.9 pad_maximum_fusion
  667.2 3.7 constant_dynamic-slice_fusion.1
  671.0 1.6 copy.32
  672.6 117.6 %while.30 = (s32[]{:T(128)}, f32[16,256]{1,0:T(8,128)S(1)}, f32[16,256]{1,0:T(8,128)S(1)}, f32[16,256,128]{1,2,0:T(8,128)}, s32[16]{0:T(128)S(1)}, /*index=5*/bf...) while((s32[]{:T(128)}, f32[16,256]{1,0:T(8,128)S(1)}, ...), condition=%wide.region_8.9_spmd.clone, body=%wide.region_5.8_spmd.clone.sunk | while | flops 69074456 | bytes 2051519 | solution.py:75
  677.6 1.9 fusion.51
  684.9 1.9 fusion.51
  692.3 1.9 fusion.51
  699.6 1.9 fusion.51
  707.0 1.9 fusion.51
  714.3 1.9 fusion.51
  721.7 1.9 fusion.51
  729.0 1.9 fusion.51
  736.4 1.9 fusion.51
  743.7 1.9 fusion.51
  751.1 1.9 fusion.51
  758.4 1.9 fusion.51
  765.8 1.9 fusion.51
  773.1 1.9 fusion.51
  780.4 1.9 fusion.51
  787.8 1.9 fusion.51
  790.1 301.6 %pmax.7 = f32[256,16]{0,1:T(8,128)S(1)} all-reduce(f32[256,16]{0,1:T(8,128)S(1)} %bitcast.67), channel_id=1, replica_groups=mesh['ctx'=64,'head'=4] {'ctx'}, use_global_device_ids=true, to_apply=%region_9.10 | all-reduce | flops 4096 | bytes 32768 | tf_op jit(solution)/shard_map/pmax | solution.py:82
  1091.8 3.1 bitcast_multiply_fusion
  1094.9 107.6 %while.29 = (s32[]{:T(128)}, bf16[16,512,128]{2,1,0:T(8,128)(2,1)S(1)}, s32[16]{0:T(128)S(1)}, bf16[512,2048]{1,0:T(8,128)(2,1)}, bf16[1024,256]{1,0:T(8,128)(2,...) while((s32[]{:T(128)}, ...), condition=%wide.region_4.5_spmd, body=%wide.region_1.4_spmd.sunk | while | flops 274332704 | bytes 10758583 | solution.py:56
  1098.6 1.6 select_reduce_fusion.4
  1105.4 1.6 select_reduce_fusion.4
  1112.1 1.6 select_reduce_fusion.4
  1118.8 1.6 select_reduce_fusion.4
  1125.5 1.6 select_reduce_fusion.4
  1132.2 1.6 select_reduce_fusion.4
  1139.0 1.6 select_reduce_fusion.4
  1145.7 1.6 select_reduce_fusion.4
  1152.4 1.6 select_reduce_fusion.4
  1159.1 1.6 select_reduce_fusion.4
  1165.9 1.6 select_reduce_fusion.4
  1172.6 1.6 select_reduce_fusion.4
  1179.3 1.6 select_reduce_fusion.4
  1186.0 1.6 select_reduce_fusion.4
  1192.7 1.6 select_reduce_fusion.4
  1199.5 1.6 select_reduce_fusion.4
  1202.5 300.9 %all-reduce.3 = f32[256,16]{0,1:T(8,128)S(1)} all-reduce(f32[256,16]{0,1:T(8,128)S(1)} %get-tuple-element.275), channel_id=3, replica_groups=mesh['ctx'=64,'head'=4] {'ctx'}, use_global_device_ids=true, to_apply=%region_11.12.clone | all-reduce | flops 4096 | bytes 32768
  1503.4 338.9 %all-reduce.9.cloned.1.call-done = f32[256,2048]{0,1:T(8,128)} async-done(((f32[256,2048]{0,1:T(8,128)}), f32[256,2048]{0,1:T(8,128)}) %all-reduce.9.cloned.1.call-update) | async-done | bytes 2097168
  1842.4 1.6 fusion.33
  1846.4 48.9 %all-to-all-start = ((bf16[4,2,1024]{2,1,0:T(2,128)(2,1)}), bf16[4,2,1024]{2,1,0:T(2,128)(2,1)S(1)}, u32[]{:S(2)}, u32[]{:S(2)}) async-start(bf16[4,2,1024]{2,1,0:T(2,128)(2,1)} %reshape.47), calls=%async_computation | async-start | bytes 32768 | tf_op jit(solution)/shard_map/all_to_all | solution.py:93
  1895.3 1.6 copy_bitcast_fusion
  1896.9 1.5 all-to-all-done
  (193 shorter events, 73.3 us)
Async XLA Ops:
  8.0 4.4 copy-start.2
  8.0 656.3 %all-reduce.7.cloned.1.call-start = ((), (), s32[]{:S(2)}) async-start(), calls=%async_computation.1 | async-start | bytes 1048576 | tf_op jit(solution)/shard_map/psum | solution.py:15
  10.0 655.3 %copy-start = (bf16[512,256]{1,0:T(8,128)(2,1)S(1)}, bf16[512,256]{1,0:T(8,128)(2,1)}, u32[]{:S(2)}) copy-start(bf16[512,256]{1,0:T(8,128)(2,1)} %param.11) | copy-start | bytes 786436
  10.0 657.2 %all-gather.3.cloned.1.call-start = ((), (), s32[]{:S(2)}) async-start(), calls=%async_computation.2 | async-start | bytes 8421376 | tf_op jit(solution)/shard_map/all_gather | solution.py:58
  10.6 1831.7 %all-reduce.9.cloned.1.call-start = ((), (), s32[]{:S(2)}) async-start(), calls=%async_computation.3 | async-start | bytes 4194304
  1098.6 2.3 copy-start.1
  1105.3 2.3 copy-start.1
  1112.1 2.3 copy-start.1
  1118.8 2.3 copy-start.1
  1125.5 2.3 copy-start.1
  1132.2 2.3 copy-start.1
  1139.0 2.3 copy-start.1
  1145.7 2.3 copy-start.1
  1152.4 2.3 copy-start.1
  1159.1 2.3 copy-start.1
  1165.8 2.3 copy-start.1
  1172.6 2.3 copy-start.1
  1179.3 2.3 copy-start.1
  1186.0 2.3 copy-start.1
  1192.7 2.3 copy-start.1
  1199.5 2.3 copy-start.1
  1846.4 52.0 %all-to-all-start = ((bf16[4,2,1024]{2,1,0:T(2,128)(2,1)}), bf16[4,2,1024]{2,1,0:T(2,128)(2,1)S(1)}, u32[]{:S(2)}, u32[]{:S(2)}) async-start(bf16[4,2,1024]{2,1,0:T(2,128)(2,1)} %reshape.47), calls=%async_computation | async-start | bytes 32768 | tf_op jit(solution)/shard_map/all_to_all | solution.py:93
Sparse Core Ops, SparseCore 0:
  11.4 652.7 all-reduce.6
  1095.0 747.3 all-reduce.8
Sparse Core Ops, SparseCore 1:
  12.6 424.6 all-gather.2
where the time goes:
time: 1910 us
  waiting for transfers between devices  909 us (48%)
  blocking collectives  685 us (36%)
  loops' own time  102 us (5%)
  matrix products  86 us (5%)
  starting transfers between devices  49 us (3%)
  local copies, waits for them, and re-layouts  31.9 us (2%)
  other arithmetic  25.9 us (1%)
    psum x1, waiting for transfers between devices, broadcast(): return lax.psum(kept, axis)  568 us
    unnamed x2, blocking collectives  383 us
    unnamed x4, waiting for transfers between devices  339 us
    pmax x1, blocking collectives, on_device(): overall = lax.pmax(highest, 'ctx')  302 us
    another operation x1, loops' own time, on_device(): lax.map(phase_two, jnp.arange(heads_here, dtype=jnp.int32))  51.9 us
    another operation x1, loops' own time, on_device(): head_outputs = lax.map(phase_one, jnp.arange(heads_here, dtype=jnp.int32))  50.2 us
    all_to_all x1, starting transfers between devices, on_device(): lax.all_to_all(merged_rows, 'head', split_axis=0, concat_axis=1, tiled=True)  48.9 us
    dot_general x32, matrix products, head_terms(): jnp.einsum('qd,kd->qk', queries, key_block, preferred_element_type=jnp.fl...  43.6 us
  transfers between devices with their start and end apart: 4, of which 3 were waited for; matrix products, arithmetic and copies ran while one was open for 3% of the time, Pallas kernels for 0%

commit v1 on v0

v1 whole, which is shorter than its diff:
```python
import functools
import math

import jax
import jax.numpy as jnp
from jax import lax
from jax.experimental import pallas as pl
from jax.experimental.pallas import tpu as pltpu
from jax.sharding import Mesh, PartitionSpec as P

DH = 128
KV_HEADS_HERE = 2
GROUP = 8
BLK = 512
NZ, NXH, NY, NXL, NCORE = 8, 2, 4, 2, 2
PEERS = NZ * NXH * NXL * NCORE
ROWS = PEERS
QUARTER = BLK // NY
EXPONENT = math.log2(math.e) / math.sqrt(DH)
HIDDEN = -1e30
FLOOR = -1e29
CTX = ("z", "xh", "y")
ZX = ("z", "xh")
HEAD = ("xl", "core")
PLANE = ("z", "xh", "xl", "core")
BF16 = jnp.bfloat16
F32 = jnp.float32


def dot_keys(queries, keys):
    return lax.dot_general(queries, keys, (((1,), (1,)), ((), ())), preferred_element_type=F32)


def dot_values(probs, values):
    return jnp.dot(probs, values, preferred_element_type=F32)


def block_kernel(heads, chunk, stack, valid_ref, q_ref, k_ref, v_ref, a0, a1, a2, a3, o_ref, keys, values):
    @pl.when(pl.program_id(1) == 0)
    def _():
        valid = valid_ref[0]
        seen = (lax.axis_index("z") + lax.axis_index("xh") + lax.axis_index("y")) > 0
        keep = lax.broadcasted_iota(jnp.int32, (BLK, DH), 0) < valid
        base = k_ref[0:1, :].astype(F32)
        keys[BLK:, :] = jnp.where(keep, k_ref[...].astype(F32), base).astype(BF16)
        values[BLK:, :DH] = jnp.where(keep, v_ref[...].astype(F32), 0.0).astype(BF16)
        values[BLK:, DH:] = jnp.where(keep, 1.0, 0.0).astype(BF16)
        for i, piece in enumerate((a0, a1, a2, a3)):
            rows = slice(QUARTER * i, QUARTER * (i + 1))
            keys[rows, :] = jnp.where(seen, piece[0:QUARTER, :].astype(F32), base).astype(BF16)
            values[rows, :DH] = jnp.where(seen, piece[QUARTER:, :].astype(F32), 0.0).astype(BF16)
        values[0:BLK, DH:] = jnp.where(seen, jnp.ones((BLK, DH), F32), 0.0).astype(BF16)

    rows = stack * chunk
    row = lax.broadcasted_iota(jnp.int32, (rows, chunk), 0) & (chunk - 1)
    causal = lax.broadcasted_iota(jnp.int32, (rows, chunk), 1) <= row
    items = [(h, r) for h in range(0, heads, stack) for r in range(BLK // chunk)]

    def scores(h, r):
        q = [q_ref[r * chunk : (r + 1) * chunk, (h + i) * DH : (h + i + 1) * DH] for i in range(stack)]
        q = q[0] if stack == 1 else jnp.concatenate(q, axis=0)
        return dot_keys(q, keys[0 : BLK + (r + 1) * chunk, :])

    def finish(h, r, s):
        n = BLK + r * chunk
        tail = jnp.where(causal, s[:, n:], HIDDEN)
        full = s[:, :n]
        top = jnp.maximum(jnp.max(full, axis=1, keepdims=True), jnp.max(tail, axis=1, keepdims=True))
        probs = jnp.concatenate(
            [jnp.exp2((full - top) * EXPONENT).astype(BF16), jnp.exp2((tail - top) * EXPONENT).astype(BF16)], axis=1
        )
        acc = dot_values(probs, values[0 : n + chunk, :])
        out = (acc[:, :DH] / acc[:, DH:]).astype(BF16)
        for i in range(stack):
            o_ref[r * chunk : (r + 1) * chunk, (h + i) * DH : (h + i + 1) * DH] = out[i * chunk : (i + 1) * chunk]

    s = scores(*items[0])
    for n, item in enumerate(items):
        following = scores(*items[n + 1]) if n + 1 < len(items) else None
        finish(*item, s)
        s = following


def block_attention(valid, q, k, v, pieces, heads=8, chunk=128, stack=2):
    steps = GROUP // heads
    kv = pl.BlockSpec((BLK, DH), lambda g, i: (0, g))
    piece = pl.BlockSpec((2 * QUARTER, DH), lambda g, i: (0, g))
    q_spec = pl.BlockSpec((BLK, heads * DH), lambda g, i: (0, g * steps + i))
    return pl.pallas_call(
        functools.partial(block_kernel, heads, chunk, stack),
        grid=(KV_HEADS_HERE, steps),
        in_specs=[pl.BlockSpec(memory_space=pltpu.SMEM), q_spec, kv, kv, piece, piece, piece, piece],
        out_specs=q_spec,
        scratch_shapes=[pltpu.VMEM((2 * BLK, DH), BF16), pltpu.VMEM((2 * BLK, 2 * DH), BF16)],
        out_shape=jax.ShapeDtypeStruct(q.shape, BF16),
        compiler_params=pltpu.CompilerParams(vmem_limit_bytes=40 << 20),
        cost_estimate=pl.CostEstimate(flops=4_000_000_000, bytes_accessed=5 << 20, transcendentals=7 << 20),
        name="block_attention",
    )(valid, q, k, v, *pieces)


def rows_kernel(chunk, valid_ref, msg_ref, k_ref, v_ref, m1, m2, m3, o_ref, keys, values):
    my_y = lax.axis_index("y")
    first = (lax.axis_index("z") * NXH + lax.axis_index("xh")) * NY
    valids, bases = [valid_ref[0].astype(F32)], [(first + my_y) * BLK]
    for message, step in ((m1, 3), (m2, 1), (m3, 2)):
        digits = message[2 * BLK :, :].astype(F32)
        valids.append(digits[0:1, 0:1] * 256.0 + digits[0:1, DH : DH + 1])
        bases.append((first + lax.rem(my_y + step, NY)) * BLK)
    arrived = msg_ref[...].astype(F32)
    limits_in = arrived[:, 16:24, :].reshape(ROWS * GROUP, DH)
    offsets = limits_in[:, 0:1] * 256.0 + limits_in[:, 64:65]
    limits = [jnp.minimum(offsets - base.astype(F32), v) for base, v in zip(bases, valids)]
    columns = lax.broadcasted_iota(jnp.int32, (chunk, BLK), 1).astype(F32)
    values[:, DH:] = jnp.ones((NY * BLK, DH), BF16)
    outs, sums = [], []
    for g in range(KV_HEADS_HERE):
        lanes = slice(g * DH, (g + 1) * DH)
        keys[0:BLK, :] = k_ref[:, lanes]
        values[0:BLK, :DH] = v_ref[:, lanes]
        for i, message in enumerate((m1, m2, m3)):
            rows = slice((i + 1) * BLK, (i + 2) * BLK)
            keys[rows, :] = message[0:BLK, lanes]
            values[rows, :DH] = message[BLK : 2 * BLK, lanes]
        queries = arrived[:, 8 * g : 8 * g + 8, :].reshape(ROWS * GROUP, DH).astype(BF16)
        parts, logs = [], []
        for r in range(0, ROWS * GROUP, chunk):
            s = dot_keys(queries[r : r + chunk], keys[...])
            pieces = [
                jnp.where(columns < limits[b][r : r + chunk], s[:, b * BLK : (b + 1) * BLK], HIDDEN) for b in range(NY)
            ]
            top = jnp.max(functools.reduce(jnp.maximum, pieces), axis=1, keepdims=True)
            top = jnp.maximum(top, FLOOR)
            probs = jnp.concatenate([jnp.exp2((p - top) * EXPONENT).astype(BF16) for p in pieces], axis=1)
            acc = dot_values(probs, values[...])
            total = acc[:, DH:]
            some = total > 0.0
            parts.append(acc[:, :DH] / jnp.where(some, total, 1.0))
            logs.append(jnp.where(some, top * EXPONENT + jnp.log2(jnp.where(some, total, 1.0)), HIDDEN))
        outs.append(jnp.concatenate(parts, axis=0).reshape(ROWS, GROUP, DH))
        sums.append(jnp.concatenate(logs, axis=0))
    lane = lax.broadcasted_iota(jnp.int32, (ROWS * GROUP, DH), 1)
    log = jnp.where(lane < 64, sums[0], sums[1])
    high = log.astype(BF16).astype(F32)
    middle = (log - high).astype(BF16).astype(F32)
    low = log - high - middle
    lane = lane & 63
    log = jnp.where(lane == 0, high, jnp.where(lane == 1, middle, low)).reshape(ROWS, GROUP, DH)
    o_ref[...] = jnp.concatenate(outs + [log], axis=1).astype(BF16)


def rows_attention(valid, msg, k, v, others, chunk=128):
    whole = pl.BlockSpec(memory_space=pltpu.VMEM)
    return pl.pallas_call(
        functools.partial(rows_kernel, chunk),
        in_specs=[pl.BlockSpec(memory_space=pltpu.SMEM)] + [whole] * 6,
        out_specs=whole,
        scratch_shapes=[pltpu.VMEM((NY * BLK, DH), BF16), pltpu.VMEM((NY * BLK, 2 * DH), BF16)],
        out_shape=jax.ShapeDtypeStruct(msg.shape, BF16),
        compiler_params=pltpu.CompilerParams(vmem_limit_bytes=40 << 20),
        cost_estimate=pl.CostEstimate(flops=1_100_000_000, bytes_accessed=3 << 20, transcendentals=2 << 20),
        name="rows_attention",
    )(valid, msg, k, v, *others)


def merge_kernel(msg_ref, o_ref):
    arrived = msg_ref[...].astype(F32).reshape(NZ * NXH, NXL * NCORE, 24, DH)
    for h in range(NXL * NCORE):
        for g in range(KV_HEADS_HERE):
            digits = arrived[:, h, 16:24, :]
            at = 64 * g
            log = digits[:, :, at : at + 1] + digits[:, :, at + 1 : at + 2] + digits[:, :, at + 2 : at + 3]
            factor = jnp.exp2(log - jnp.max(log, axis=0, keepdims=True))
            total = jnp.sum(factor, axis=0)
            merged = jnp.sum(factor * arrived[:, h, 8 * g : 8 * g + 8, :], axis=0) / total
            start = (h * KV_HEADS_HERE + g) * GROUP
            o_ref[start : start + GROUP, :] = merged


def merge(msg):
    whole = pl.BlockSpec(memory_space=pltpu.VMEM)
    return pl.pallas_call(
        merge_kernel,
        in_specs=[whole],
        out_specs=whole,
        out_shape=jax.ShapeDtypeStruct((NXL * NCORE * KV_HEADS_HERE * GROUP, DH), F32),
        name="merge",
    )(msg)


def shift(n, by):
    return [(i, (i + by) % n) for i in range(n)]


def digits_of(number):
    high = number // 256
    return high.astype(BF16), (number - high * 256).astype(BF16)


def place(z, xh):
    return (z % NZ) * NXH + xh


def to_ring(array):
    return [lax.ppermute(array, "y", shift(NY, by)) for by in (1, -1, 2)]


def spread_anchor(kv):
    quarters = [jnp.concatenate([kv[r : r + QUARTER], kv[BLK + r : BLK + r + QUARTER]]) for r in range(0, BLK, QUARTER)]
    current = jnp.where(lax.axis_index(CTX) == 0, quarters[0], jnp.zeros_like(quarters[0]))
    for y in range(1, NY):
        current = current + lax.ppermute(quarters[y], CTX, [(0, y)])
    sent = [lax.ppermute(current, ZX, [(0, place(z, 0))]) for z in (2, 4, 6)]
    current = current + sent[0] + sent[1] + sent[2]
    even = (0, 2, 4, 6)
    sent = [
        lax.ppermute(current, ZX, [(place(z, 0), place(z + dz, xh)) for z in even]) for dz, xh in ((0, 1), (1, 0), (1, 1))
    ]
    current = current + sent[0] + sent[1] + sent[2]
    return [current] + to_ring(current)


def on_device(ctx_query, ctx_key, ctx_value, valid, query_rows, offsets):
    high, low = digits_of(valid)
    extra = jnp.concatenate([jnp.broadcast_to(high[None], (16, DH)), jnp.broadcast_to(low[None], (16, DH))], axis=1)
    kv = jnp.concatenate([ctx_key, ctx_value, extra], axis=0)
    others = to_ring(kv)

    high, low = digits_of(offsets)
    limit = jnp.concatenate(
        [jnp.broadcast_to(high[None, None], (4, 8, 64)), jnp.broadcast_to(low[None, None], (4, 8, 64))], axis=2
    )
    message = jnp.concatenate([query_rows.reshape(4, 16, DH), limit], axis=1)
    message = jnp.broadcast_to(message[None], (NZ * NXH, 4, 24, DH)).reshape(PEERS, 24, DH)
    message = lax.all_to_all(message, PLANE, 0, 0, tiled=True)

    pieces = spread_anchor(kv)
    partial = rows_attention(valid, message, ctx_key, ctx_value, others)
    partial = lax.all_to_all(partial, PLANE, 0, 0, tiled=True)
    block_out = block_attention(valid, ctx_query, ctx_key, ctx_value, pieces)
    query_out = merge(partial).astype(BF16).reshape(1, -1)
    return (block_out, query_out)


def solution(mesh):
    fine = Mesh(mesh.devices.reshape(NZ, NXH, NY, NXL, NCORE), ("z", "xh", "y", "xl", "core"))
    return jax.shard_map(
        on_device,
        mesh=fine,
        in_specs=(P(CTX, HEAD), P(CTX, HEAD), P(CTX, HEAD), P(CTX), P(CTX + HEAD, None), P(CTX + HEAD)),
        out_specs=(P(CTX, HEAD), P(CTX + HEAD, None)),
        check_vma=False,
    )
```

time: 1910 us -> 97.6 us (0.05)
  waiting for transfers between devices: 909 us -> 21.1 us
  blocking collectives: 685 us -> 0 us
  loops' own time: 102 us -> 0 us
  matrix products: 86 us -> 0 us
  local copies, waits for them, and re-layouts: 31.9 us -> 5.95 us
  other arithmetic: 25.9 us -> 5.26 us
    psum x1 -> x0, waiting for transfers between devices: 568 us -> none  [broadcast(): return lax.psum(kept, axis)]
    unnamed x2 -> x0, blocking collectives: 383 us -> none
    unnamed x4 -> x0, waiting for transfers between devices: 339 us -> none
    pmax x1 -> x0, blocking collectives: 302 us -> none  [on_device(): overall = lax.pmax(highest, 'ctx')]
    another operation x2 -> x0, loops' own time: 102 us -> none  [the longest x1 51.9 us: on_device(): lax.map(phase_two, jnp.arange(heads_here, dtype=jnp.int32))]
    dot_general x64 -> x0, matrix products: 86 us -> none  [the longest x32 43.6 us: head_terms(): jnp.einsum('qd,kd->qk', queries, key_block, preferred_element_type=jnp.fl...]
    all_to_all x1 -> x2, starting transfers between devices: 48.9 us -> 21.1 us  [the longest x1 13 us: on_device(): message = lax.all_to_all(message, PLANE, 0, 0, tiled=True)]
    ppermute x0 -> x15, starting transfers between devices: none -> 24.1 us  [the longest x3 8.73 us: spread_anchor(): current = current + lax.ppermute(quarters[y], CTX, [(0, y)])]
  transfers between devices with their start and end apart: 4 -> 17, of which waited for: 3 -> 5; matrix products, arithmetic and copies ran while one was open for 3% -> 4% of each run, Pallas kernels for 0% -> 15%
where the time goes in v1:
time: 97.6 us; the launch traced here: 96.8 us
  starting transfers between devices  45.3 us (46%)
  waiting for transfers between devices  21.1 us (22%)
  Pallas kernels  17 us (17%)
  local copies, waits for them, and re-layouts  5.95 us (6%)
  other arithmetic  5.26 us (5%)
  between operations  2.29 us (2%)
    all_to_all x1, starting transfers between devices, on_device(): message = lax.all_to_all(message, PLANE, 0, 0, tiled=True)  13 us
    ppermute x3, waiting for transfers between devices, spread_anchor(): current = current + lax.ppermute(quarters[y], CTX, [(0, y)])  11.4 us
    pallas_call x1, Pallas kernels, block_attention(): pl.pallas_call(functools.partial(block_kernel, heads, chunk, stack), grid...  10.2 us
    ppermute x3, starting transfers between devices, spread_anchor(): current = current + lax.ppermute(quarters[y], CTX, [(0, y)])  8.73 us
    all_to_all x1, starting transfers between devices, on_device(): partial = lax.all_to_all(partial, PLANE, 0, 0, tiled=True)  8.15 us
    ppermute x6, waiting for transfers between devices, to_ring(): return [lax.ppermute(array, 'y', shift(NY, by)) for by in (1, -1, 2)]  6.01 us
    ppermute x3, starting transfers between devices, spread_anchor(): lax.ppermute(current, ZX, [(place(z, 0), place(z + dz, xh)) for z in even])  5.82 us
    ppermute x6, starting transfers between devices, to_ring(): return [lax.ppermute(array, 'y', shift(NY, by)) for by in (1, -1, 2)]  5.69 us
  transfers between devices with their start and end apart: 17, of which 5 were waited for; matrix products, arithmetic and copies ran while one was open for 4% of the time, Pallas kernels for 15%

profile of v1, /device:TPU:1, one launch (start us, length us, event | category | flops | bytes accessed | tf_op | source)
XLA Modules:
  0.0 96.8 jit_solution(11309449919850269187)
XLA Ops:
  1.4 0.8 reduce
  2.3 0.8 broadcast_in_dim.20
  3.1 13.0 %all-to-all-start = ((bf16[64,24,128]{2,1,0:T(8,128)(2,1)}), bf16[64,24,128]{2,1,0:T(8,128)(2,1)S(1)}, u32[]{:S(2)}, u32[]{:S(2)}) async-start(bf16[64,24,128]{2,1,0:T(8,128)(2,1)} %bitcast.2), calls=%async_computation | async-start | bytes 786432 | tf_op jit(solution)/shard_map/all_to_all | solution.py:235
  16.2 3.9 %collective-permute-start = (bf16[256,256]{1,0:T(8,128)(2,1)S(1)}, bf16[256,256]{1,0:T(8,128)(2,1)}, u32[]{:S(2)}, u32[]{:S(2)}) collective-permute-start(bf16[256,256]{1,0:T(8,128)(2,1)S(1)} %pad_maximum_fusion.1), channel_id=1, source_target_pairs={{0,4},{1,5},{2,6},{3,7}} | collective-permute-start | bytes 393224 | tf_op jit(solution)/shard_map/ppermute | solution.py:212
  20.0 2.9 %collective-permute-start.1 = (bf16[256,256]{1,0:T(8,128)(2,1)S(1)}, bf16[256,256]{1,0:T(8,128)(2,1)}, u32[]{:S(2)}, u32[]{:S(2)}) collective-permute-start(bf16[256,256]{1,0:T(8,128)(2,1)S(1)} %pad_maximum_fusion.2), channel_id=1, source_target_pairs={{0,8},{1,9},{2,10},{3,11}} | collective-permute-start | bytes 393224 | tf_op jit(solution)/shard_map/ppermute | solution.py:212
  23.0 0.7 pad_maximum_fusion.3
  23.6 1.9 %collective-permute-start.2 = (bf16[256,256]{1,0:T(8,128)(2,1)}, bf16[256,256]{1,0:T(8,128)(2,1)}, u32[]{:S(2)}, u32[]{:S(2)}) collective-permute-start(bf16[256,256]{1,0:T(8,128)(2,1)} %pad_maximum_fusion.3), channel_id=1, source_target_pairs={{0,12},{1,13},{2,14},{3,15}} | collective-permute-start | bytes 393224 | tf_op jit(solution)/shard_map/ppermute | solution.py:212
  26.3 0.1 collective-permute-start.14
  26.4 0.1 collective-permute-start.13
  26.5 0.0 collective-permute-done
  26.5 1.4 %collective-permute-start.12 = (bf16[1040,256]{1,0:T(8,128)(2,1)S(1)}, bf16[1040,256]{1,0:T(8,128)(2,1)S(1)}, u32[]{:S(2)}, u32[]{:S(2)}) collective-permute-start(bf16[1040,256]{1,0:T(8,128)(2,1)S(1)} %pad_maximum_fusion), channel_id=1, source_target_pairs={{0,4},{4,8},{8,12},{12,0},{1,5},{5,9},{9,13},{13,1},{2,6},{6,10},{... | collective-permute-start | bytes 1597448 | tf_op jit(solution)/shard_map/ppermute | solution.py:205
  28.0 0.0 collective-permute-done.1
  28.0 11.4 %collective-permute-done.2 = bf16[256,256]{1,0:T(8,128)(2,1)} collective-permute-done((bf16[256,256]{1,0:T(8,128)(2,1)}, bf16[256,256]{1,0:T(8,128)(2,1)}, u32[]{:S(2)}, u32[]{:S(2)}) %collective-permute-start.2) | collective-permute-done | bytes 131104 | tf_op jit(solution)/shard_map/ppermute | solution.py:212
  39.4 1.1 %fusion.2 = bf16[256,256]{1,0:T(8,128)(2,1)S(1)} fusion(bf16[256,256]{1,0:T(8,128)(2,1)} %collective-permute-done.2, bf16[256,256]{1,0:T(8,128)(2,1)} %collective-permute-done.1, bf16[256,256]{1,0:T(8,128)(2,1)} %collective-permute-done, bf16[128,256]{1,0:T(8,128)(2,1)S(1)} %get-tuple-element.13, bf16[128,256]{1,0:T(8,128)(2,1)S(1)} %get-tuple-element.2, ...), kind=kLoop, calls=%fused_computation.4 | loop fusion | flops 851968 | bytes 655361 | tf_op jit(solution)/shard_map/add | solution.py:212
  40.5 1.3 %collective-permute-start.5 = (bf16[256,256]{1,0:T(8,128)(2,1)S(1)}, bf16[256,256]{1,0:T(8,128)(2,1)S(1)}, u32[]{:S(2)}, u32[]{:S(2)}) collective-permute-start(bf16[256,256]{1,0:T(8,128)(2,1)S(1)} %fusion.2), channel_id=1, source_target_pairs={{0,192},{1,193},{2,194},{3,195},{4,196},{5,197},{6,198},{7,199},{8... | collective-permute-start | bytes 393224 | tf_op jit(solution)/shard_map/ppermute | solution.py:213
  41.8 1.3 %collective-permute-start.4 = (bf16[256,256]{1,0:T(8,128)(2,1)S(1)}, bf16[256,256]{1,0:T(8,128)(2,1)S(1)}, u32[]{:S(2)}, u32[]{:S(2)}) collective-permute-start(bf16[256,256]{1,0:T(8,128)(2,1)S(1)} %fusion.2), channel_id=1, source_target_pairs={{0,128},{1,129},{2,130},{3,131},{4,132},{5,133},{6,134},{7,135},{8... | collective-permute-start | bytes 393224 | tf_op jit(solution)/shard_map/ppermute | solution.py:213
  43.1 1.3 %collective-permute-done.5 = bf16[256,256]{1,0:T(8,128)(2,1)S(1)} collective-permute-done((bf16[256,256]{1,0:T(8,128)(2,1)S(1)}, bf16[256,256]{1,0:T(8,128)(2,1)S(1)}, u32[]{:S(2)}, u32[]{:S(2)}) %collective-permute-start.5) | collective-permute-done | bytes 131104 | tf_op jit(solution)/shard_map/ppermute | solution.py:213
  44.4 1.3 %collective-permute-start.3 = (bf16[256,256]{1,0:T(8,128)(2,1)S(1)}, bf16[256,256]{1,0:T(8,128)(2,1)S(1)}, u32[]{:S(2)}, u32[]{:S(2)}) collective-permute-start(bf16[256,256]{1,0:T(8,128)(2,1)S(1)} %fusion.2), channel_id=1, source_target_pairs={{0,64},{1,65},{2,66},{3,67},{4,68},{5,69},{6,70},{7,71},{8,72},{9,... | collective-permute-start | bytes 393224 | tf_op jit(solution)/shard_map/ppermute | solution.py:213
  45.7 0.0 collective-permute-done.4
  45.7 2.4 %collective-permute-done.3 = bf16[256,256]{1,0:T(8,128)(2,1)S(1)} collective-permute-done((bf16[256,256]{1,0:T(8,128)(2,1)S(1)}, bf16[256,256]{1,0:T(8,128)(2,1)S(1)}, u32[]{:S(2)}, u32[]{:S(2)}) %collective-permute-start.3) | collective-permute-done | bytes 131104 | tf_op jit(solution)/shard_map/ppermute | solution.py:213
  48.1 0.7 add_add_fusion.1
  48.8 1.9 %collective-permute-start.8 = (bf16[256,256]{1,0:T(8,128)(2,1)}, bf16[256,256]{1,0:T(8,128)(2,1)}, u32[]{:S(2)}, u32[]{:S(2)}) collective-permute-start(bf16[256,256]{1,0:T(8,128)(2,1)} %add_add_fusion.1), channel_id=1, source_target_pairs={{0,48},{64,112},{128,176},{192,240},{1,49},{65,113},{129,177},{193... | collective-permute-start | bytes 393224 | tf_op jit(solution)/shard_map/ppermute | solution.py:217
  50.7 1.9 %collective-permute-start.7 = (bf16[256,256]{1,0:T(8,128)(2,1)}, bf16[256,256]{1,0:T(8,128)(2,1)}, u32[]{:S(2)}, u32[]{:S(2)}) collective-permute-start(bf16[256,256]{1,0:T(8,128)(2,1)} %add_add_fusion.1), channel_id=1, source_target_pairs={{0,32},{64,96},{128,160},{192,224},{1,33},{65,97},{129,161},{193,2... | collective-permute-start | bytes 393224 | tf_op jit(solution)/shard_map/ppermute | solution.py:217
  52.7 0.0 collective-permute-done.14.m3
  52.7 1.9 %collective-permute-start.6 = (bf16[256,256]{1,0:T(8,128)(2,1)}, bf16[256,256]{1,0:T(8,128)(2,1)}, u32[]{:S(2)}, u32[]{:S(2)}) collective-permute-start(bf16[256,256]{1,0:T(8,128)(2,1)} %add_add_fusion.1), channel_id=1, source_target_pairs={{0,16},{64,80},{128,144},{192,208},{1,17},{65,81},{129,145},{193,2... | collective-permute-start | bytes 393224 | tf_op jit(solution)/shard_map/ppermute | solution.py:217
  54.6 0.0 collective-permute-done.13.m2
  54.6 0.8 copy-done.3
  55.4 0.0 collective-permute-done.12.m1
  55.4 0.8 copy-done.5
  56.2 0.0 all-to-all-done.msg_ref
  56.2 1.0 %copy-done.4 = bf16[1040,256]{1,0:T(8,128)(2,1)S(1)} copy-done((bf16[1040,256]{1,0:T(8,128)(2,1)S(1)}, bf16[1040,256]{1,0:T(8,128)(2,1)}, u32[]{:S(2)}) %copy-start.4) | copy-done | bytes 532504
  57.3 1.0 %copy-done.6 = bf16[1040,256]{1,0:T(8,128)(2,1)S(1)} copy-done((bf16[1040,256]{1,0:T(8,128)(2,1)S(1)}, bf16[1040,256]{1,0:T(8,128)(2,1)}, u32[]{:S(2)}) %copy-start.6) | copy-done | bytes 532504
  58.3 4.5 %rows_attention.1 = bf16[64,24,128]{2,1,0:T(8,128)(2,1)} custom-call(s32[1]{0:T(128)S(6)} %copy.11.valid_ref, bf16[64,24,128]{2,1,0:T(8,128)(2,1)S(1)} %all-to-all-done.msg_ref, bf16[512,256]{1,0:T(8,128)(2,1)S(1)} %copy-done, bf16[512,256]{1,0:T(8,128)(2,1)S(1)} %copy-done.1, bf16[1040,256]{1,0:T(8,128)(2,1)S(1)} %copy-done.6, ...), custom_call_target="tpu_custom_call" | custom-call | flops 1100000000 | bytes 3145728 | tf_op jit(solution)/shard_map/rows_attention/pallas_call | solution.py:154
  62.9 8.2 %all-to-all-start.1 = ((bf16[64,24,128]{2,1,0:T(8,128)(2,1)}), bf16[64,24,128]{2,1,0:T(8,128)(2,1)S(1)}, u32[]{:S(2)}, u32[]{:S(2)}) async-start(bf16[64,24,128]{2,1,0:T(8,128)(2,1)} %rows_attention.1), calls=%async_computation.1 | async-start | bytes 786432 | tf_op jit(solution)/shard_map/all_to_all | solution.py:239
  71.1 0.0 collective-permute-done.7
  71.1 1.1 %add_add_fusion.a0 = bf16[256,256]{1,0:T(8,128)(2,1)S(1)} fusion(bf16[256,256]{1,0:T(8,128)(2,1)} %collective-permute-done.8, bf16[256,256]{1,0:T(8,128)(2,1)} %collective-permute-done.7, bf16[256,256]{1,0:T(8,128)(2,1)} %add_add_fusion.1, bf16[256,256]{1,0:T(8,128)(2,1)} %collective-permute-done.6), kind=kLoop, calls=%fused_computation.8 | loop fusion | flops 196608 | bytes 655360 | tf_op jit(solution)/shard_map/add | solution.py:219
  72.2 0.1 collective-permute-start.11
  72.3 3.5 %collective-permute-start.10 = (bf16[256,256]{1,0:T(8,128)(2,1)S(1)}, bf16[256,256]{1,0:T(8,128)(2,1)S(1)}, u32[]{:S(2)}, u32[]{:S(2)}) collective-permute-start(bf16[256,256]{1,0:T(8,128)(2,1)S(1)} %add_add_fusion.a0), channel_id=1, source_target_pairs={{0,12},{4,0},{8,4},{12,8},{1,13},{5,1},{9,5},{13,9},{2,14},{6,2},{... | collective-permute-start | bytes 393224 | tf_op jit(solution)/shard_map/ppermute | solution.py:205
  75.8 0.5 collective-permute-start.9
  76.3 2.1 %collective-permute-done.11.a3 = bf16[256,256]{1,0:T(8,128)(2,1)S(1)} collective-permute-done((bf16[256,256]{1,0:T(8,128)(2,1)S(1)}, bf16[256,256]{1,0:T(8,128)(2,1)S(1)}, u32[]{:S(2)}, u32[]{:S(2)}) %collective-permute-start.11) | collective-permute-done | bytes 131104 | tf_op jit(solution)/shard_map/ppermute | solution.py:205
  78.4 3.9 %collective-permute-done.10.a2 = bf16[256,256]{1,0:T(8,128)(2,1)S(1)} collective-permute-done((bf16[256,256]{1,0:T(8,128)(2,1)S(1)}, bf16[256,256]{1,0:T(8,128)(2,1)S(1)}, u32[]{:S(2)}, u32[]{:S(2)}) %collective-permute-start.10) | collective-permute-done | bytes 131104 | tf_op jit(solution)/shard_map/ppermute | solution.py:205
  82.3 0.0 collective-permute-done.9.a1
  82.3 10.2 %block_attention.1 = bf16[512,2048]{1,0:T(8,128)(2,1)} custom-call(s32[1]{0:T(128)S(6)} %copy.11.valid_ref, bf16[512,2048]{1,0:T(8,128)(2,1)S(1)} %copy-done.2, bf16[512,256]{1,0:T(8,128)(2,1)S(1)} %copy-done, bf16[512,256]{1,0:T(8,128)(2,1)S(1)} %copy-done.1, bf16[256,256]{1,0:T(8,128)(2,1)S(1)} %add_add_fusion.a0, ...), custom_call_target="tpu_custom_call" | custom-call | flops 4000000000 | bytes 5242880 | tf_op jit(solution)/shard_map/block_attention/pallas_call | solution.py:89
  92.5 0.0 all-to-all-done.1.msg_ref
  92.5 0.7 copy-done.7
  93.3 2.2 %merge.1 = f32[64,128]{1,0:T(8,128)} custom-call(bf16[64,24,128]{2,1,0:T(8,128)(2,1)} %copy-done.7), custom_call_target="tpu_custom_call" | custom-call | tf_op jit(solution)/shard_map/merge/pallas_call | solution.py:182
  95.4 0.8 convert_bitcast_fusion
  96.2 0.6 copy.10
  (24 shorter events, 0.2 us)
Async XLA Ops:
  0.6 15.4 %copy-start.1 = (bf16[512,256]{1,0:T(8,128)(2,1)S(1)}, bf16[512,256]{1,0:T(8,128)(2,1)}, u32[]{:S(2)}) copy-start(bf16[512,256]{1,0:T(8,128)(2,1)} %v_ref.3) | copy-start | bytes 786436
  0.6 15.4 %copy-start = (bf16[512,256]{1,0:T(8,128)(2,1)S(1)}, bf16[512,256]{1,0:T(8,128)(2,1)}, u32[]{:S(2)}) copy-start(bf16[512,256]{1,0:T(8,128)(2,1)} %k_ref.3) | copy-start | bytes 786436
  3.1 53.2 %all-to-all-start = ((bf16[64,24,128]{2,1,0:T(8,128)(2,1)}), bf16[64,24,128]{2,1,0:T(8,128)(2,1)S(1)}, u32[]{:S(2)}, u32[]{:S(2)}) async-start(bf16[64,24,128]{2,1,0:T(8,128)(2,1)} %bitcast.2), calls=%async_computation | async-start | bytes 786432 | tf_op jit(solution)/shard_map/all_to_all | solution.py:235
  16.2 10.4 %collective-permute-start = (bf16[256,256]{1,0:T(8,128)(2,1)S(1)}, bf16[256,256]{1,0:T(8,128)(2,1)}, u32[]{:S(2)}, u32[]{:S(2)}) collective-permute-start(bf16[256,256]{1,0:T(8,128)(2,1)S(1)} %pad_maximum_fusion.1), channel_id=1, source_target_pairs={{0,4},{1,5},{2,6},{3,7}} | collective-permute-start | bytes 393224 | tf_op jit(solution)/shard_map/ppermute | solution.py:212
  20.0 8.0 %collective-permute-start.1 = (bf16[256,256]{1,0:T(8,128)(2,1)S(1)}, bf16[256,256]{1,0:T(8,128)(2,1)}, u32[]{:S(2)}, u32[]{:S(2)}) collective-permute-start(bf16[256,256]{1,0:T(8,128)(2,1)S(1)} %pad_maximum_fusion.2), channel_id=1, source_target_pairs={{0,8},{1,9},{2,10},{3,11}} | collective-permute-start | bytes 393224 | tf_op jit(solution)/shard_map/ppermute | solution.py:212
  23.6 15.8 %collective-permute-start.2 = (bf16[256,256]{1,0:T(8,128)(2,1)}, bf16[256,256]{1,0:T(8,128)(2,1)}, u32[]{:S(2)}, u32[]{:S(2)}) collective-permute-start(bf16[256,256]{1,0:T(8,128)(2,1)} %pad_maximum_fusion.3), channel_id=1, source_target_pairs={{0,12},{1,13},{2,14},{3,15}} | collective-permute-start | bytes 393224 | tf_op jit(solution)/shard_map/ppermute | solution.py:212
  26.3 26.3 %collective-permute-start.14 = (bf16[1040,256]{1,0:T(8,128)(2,1)S(1)}, bf16[1040,256]{1,0:T(8,128)(2,1)S(1)}, u32[]{:S(2)}, u32[]{:S(2)}) collective-permute-start(bf16[1040,256]{1,0:T(8,128)(2,1)S(1)} %pad_maximum_fusion), channel_id=1, source_target_pairs={{0,8},{4,12},{8,0},{12,4},{1,9},{5,13},{9,1},{13,5},{2,10},{6,14},... | collective-permute-start | bytes 1597448 | tf_op jit(solution)/shard_map/ppermute | solution.py:205
  26.4 28.2 %collective-permute-start.13 = (bf16[1040,256]{1,0:T(8,128)(2,1)S(1)}, bf16[1040,256]{1,0:T(8,128)(2,1)S(1)}, u32[]{:S(2)}, u32[]{:S(2)}) collective-permute-start(bf16[1040,256]{1,0:T(8,128)(2,1)S(1)} %pad_maximum_fusion), channel_id=1, source_target_pairs={{0,12},{4,0},{8,4},{12,8},{1,13},{5,1},{9,5},{13,9},{2,14},{6,2},{... | collective-permute-start | bytes 1597448 | tf_op jit(solution)/shard_map/ppermute | solution.py:205
  26.5 28.9 %collective-permute-start.12 = (bf16[1040,256]{1,0:T(8,128)(2,1)S(1)}, bf16[1040,256]{1,0:T(8,128)(2,1)S(1)}, u32[]{:S(2)}, u32[]{:S(2)}) collective-permute-start(bf16[1040,256]{1,0:T(8,128)(2,1)S(1)} %pad_maximum_fusion), channel_id=1, source_target_pairs={{0,4},{4,8},{8,12},{12,0},{1,5},{5,9},{9,13},{13,1},{2,6},{6,10},{... | collective-permute-start | bytes 1597448 | tf_op jit(solution)/shard_map/ppermute | solution.py:205
  40.5 3.9 %collective-permute-start.5 = (bf16[256,256]{1,0:T(8,128)(2,1)S(1)}, bf16[256,256]{1,0:T(8,128)(2,1)S(1)}, u32[]{:S(2)}, u32[]{:S(2)}) collective-permute-start(bf16[256,256]{1,0:T(8,128)(2,1)S(1)} %fusion.2), channel_id=1, source_target_pairs={{0,192},{1,193},{2,194},{3,195},{4,196},{5,197},{6,198},{7,199},{8... | collective-permute-start | bytes 393224 | tf_op jit(solution)/shard_map/ppermute | solution.py:213
  41.8 3.9 %collective-permute-start.4 = (bf16[256,256]{1,0:T(8,128)(2,1)S(1)}, bf16[256,256]{1,0:T(8,128)(2,1)S(1)}, u32[]{:S(2)}, u32[]{:S(2)}) collective-permute-start(bf16[256,256]{1,0:T(8,128)(2,1)S(1)} %fusion.2), channel_id=1, source_target_pairs={{0,128},{1,129},{2,130},{3,131},{4,132},{5,133},{6,134},{7,135},{8... | collective-permute-start | bytes 393224 | tf_op jit(solution)/shard_map/ppermute | solution.py:213
  44.4 3.7 %collective-permute-start.3 = (bf16[256,256]{1,0:T(8,128)(2,1)S(1)}, bf16[256,256]{1,0:T(8,128)(2,1)S(1)}, u32[]{:S(2)}, u32[]{:S(2)}) collective-permute-start(bf16[256,256]{1,0:T(8,128)(2,1)S(1)} %fusion.2), channel_id=1, source_target_pairs={{0,64},{1,65},{2,66},{3,67},{4,68},{5,69},{6,70},{7,71},{8,72},{9,... | collective-permute-start | bytes 393224 | tf_op jit(solution)/shard_map/ppermute | solution.py:213
  48.8 22.2 %collective-permute-start.8 = (bf16[256,256]{1,0:T(8,128)(2,1)}, bf16[256,256]{1,0:T(8,128)(2,1)}, u32[]{:S(2)}, u32[]{:S(2)}) collective-permute-start(bf16[256,256]{1,0:T(8,128)(2,1)} %add_add_fusion.1), channel_id=1, source_target_pairs={{0,48},{64,112},{128,176},{192,240},{1,49},{65,113},{129,177},{193... | collective-permute-start | bytes 393224 | tf_op jit(solution)/shard_map/ppermute | solution.py:217
  50.7 20.3 %collective-permute-start.7 = (bf16[256,256]{1,0:T(8,128)(2,1)}, bf16[256,256]{1,0:T(8,128)(2,1)}, u32[]{:S(2)}, u32[]{:S(2)}) collective-permute-start(bf16[256,256]{1,0:T(8,128)(2,1)} %add_add_fusion.1), channel_id=1, source_target_pairs={{0,32},{64,96},{128,160},{192,224},{1,33},{65,97},{129,161},{193,2... | collective-permute-start | bytes 393224 | tf_op jit(solution)/shard_map/ppermute | solution.py:217
  52.7 18.4 %collective-permute-start.6 = (bf16[256,256]{1,0:T(8,128)(2,1)}, bf16[256,256]{1,0:T(8,128)(2,1)}, u32[]{:S(2)}, u32[]{:S(2)}) collective-permute-start(bf16[256,256]{1,0:T(8,128)(2,1)} %add_add_fusion.1), channel_id=1, source_target_pairs={{0,16},{64,80},{128,144},{192,208},{1,17},{65,81},{129,145},{193,2... | collective-permute-start | bytes 393224 | tf_op jit(solution)/shard_map/ppermute | solution.py:217
  54.6 0.8 copy-start.3
  55.4 0.8 copy-start.5
  56.2 1.0 %copy-start.4 = (bf16[1040,256]{1,0:T(8,128)(2,1)S(1)}, bf16[1040,256]{1,0:T(8,128)(2,1)}, u32[]{:S(2)}) copy-start(bf16[1040,256]{1,0:T(8,128)(2,1)} %copy-done.3) | copy-start | bytes 1597444
  57.3 1.0 %copy-start.6 = (bf16[1040,256]{1,0:T(8,128)(2,1)S(1)}, bf16[1040,256]{1,0:T(8,128)(2,1)}, u32[]{:S(2)}) copy-start(bf16[1040,256]{1,0:T(8,128)(2,1)} %copy-done.5) | copy-start | bytes 1597444
  58.3 24.0 %copy-start.2 = (bf16[512,2048]{1,0:T(8,128)(2,1)S(1)}, bf16[512,2048]{1,0:T(8,128)(2,1)}, u32[]{:S(2)}) copy-start(bf16[512,2048]{1,0:T(8,128)(2,1)} %q_ref.1) | copy-start | bytes 6291460
  62.9 29.6 %all-to-all-start.1 = ((bf16[64,24,128]{2,1,0:T(8,128)(2,1)}), bf16[64,24,128]{2,1,0:T(8,128)(2,1)S(1)}, u32[]{:S(2)}, u32[]{:S(2)}) async-start(bf16[64,24,128]{2,1,0:T(8,128)(2,1)} %rows_attention.1), calls=%async_computation.1 | async-start | bytes 786432 | tf_op jit(solution)/shard_map/all_to_all | solution.py:239
  72.2 6.2 %collective-permute-start.11 = (bf16[256,256]{1,0:T(8,128)(2,1)S(1)}, bf16[256,256]{1,0:T(8,128)(2,1)S(1)}, u32[]{:S(2)}, u32[]{:S(2)}) collective-permute-start(bf16[256,256]{1,0:T(8,128)(2,1)S(1)} %add_add_fusion.a0), channel_id=1, source_target_pairs={{0,8},{4,12},{8,0},{12,4},{1,9},{5,13},{9,1},{13,5},{2,10},{6,14},... | collective-permute-start | bytes 393224 | tf_op jit(solution)/shard_map/ppermute | solution.py:205
  72.3 10.0 %collective-permute-start.10 = (bf16[256,256]{1,0:T(8,128)(2,1)S(1)}, bf16[256,256]{1,0:T(8,128)(2,1)S(1)}, u32[]{:S(2)}, u32[]{:S(2)}) collective-permute-start(bf16[256,256]{1,0:T(8,128)(2,1)S(1)} %add_add_fusion.a0), channel_id=1, source_target_pairs={{0,12},{4,0},{8,4},{12,8},{1,13},{5,1},{9,5},{13,9},{2,14},{6,2},{... | collective-permute-start | bytes 393224 | tf_op jit(solution)/shard_map/ppermute | solution.py:205
  75.8 6.5 %collective-permute-start.9 = (bf16[256,256]{1,0:T(8,128)(2,1)S(1)}, bf16[256,256]{1,0:T(8,128)(2,1)S(1)}, u32[]{:S(2)}, u32[]{:S(2)}) collective-permute-start(bf16[256,256]{1,0:T(8,128)(2,1)S(1)} %add_add_fusion.a0), channel_id=1, source_target_pairs={{0,4},{4,8},{8,12},{12,0},{1,5},{5,9},{9,13},{13,1},{2,6},{6,10},{... | collective-permute-start | bytes 393224 | tf_op jit(solution)/shard_map/ppermute | solution.py:205
  92.5 0.7 copy-start.7

commit v2 on v1

--- a/solution.py
+++ b/solution.py
@@ -27,6 +27,10 @@
 F32 = jnp.float32
 
 
+SMALL = pltpu.CompilerParams(vmem_limit_bytes=6 << 20)
+LONG = pl.CostEstimate(flops=10**12, bytes_accessed=1 << 20, transcendentals=0)
+
+
 def dot_keys(queries, keys):
     return lax.dot_general(queries, keys, (((1,), (1,)), ((), ())), preferred_element_type=F32)
 
@@ -93,74 +97,94 @@
         out_specs=q_spec,
         scratch_shapes=[pltpu.VMEM((2 * BLK, DH), BF16), pltpu.VMEM((2 * BLK, 2 * DH), BF16)],
         out_shape=jax.ShapeDtypeStruct(q.shape, BF16),
-        compiler_params=pltpu.CompilerParams(vmem_limit_bytes=40 << 20),
-        cost_estimate=pl.CostEstimate(flops=4_000_000_000, bytes_accessed=5 << 20, transcendentals=7 << 20),
+        compiler_params=pltpu.CompilerParams(vmem_limit_bytes=20 << 20),
+        cost_estimate=pl.CostEstimate(flops=12_000_000_000, bytes_accessed=5 << 20, transcendentals=7 << 20),
         name="block_attention",
     )(valid, q, k, v, *pieces)
 
 
-def rows_kernel(chunk, valid_ref, msg_ref, k_ref, v_ref, m1, m2, m3, o_ref, keys, values):
+def rows_kernel(chunk, valid_ref, msg_ref, k_ref, v_ref, m1, m2, k3, v3, *rest):
+    o_ref, keys, values, sent = rest[-4:]
+    g = pl.program_id(0)
     my_y = lax.axis_index("y")
     first = (lax.axis_index("z") * NXH + lax.axis_index("xh")) * NY
     valids, bases = [valid_ref[0].astype(F32)], [(first + my_y) * BLK]
-    for message, step in ((m1, 3), (m2, 1), (m3, 2)):
-        digits = message[2 * BLK :, :].astype(F32)
-        valids.append(digits[0:1, 0:1] * 256.0 + digits[0:1, DH : DH + 1])
+    for message, step in ((m1, 3), (m2, 1), (k3, 2)):
+        digits = message[BLK : BLK + 16, :].astype(F32)
+        valids.append(digits[0:1, 0:1] * 256.0 + digits[8:9, 0:1])
         bases.append((first + lax.rem(my_y + step, NY)) * BLK)
     arrived = msg_ref[...].astype(F32)
     limits_in = arrived[:, 16:24, :].reshape(ROWS * GROUP, DH)
     offsets = limits_in[:, 0:1] * 256.0 + limits_in[:, 64:65]
     limits = [jnp.minimum(offsets - base.astype(F32), v) for base, v in zip(bases, valids)]
     columns = lax.broadcasted_iota(jnp.int32, (chunk, BLK), 1).astype(F32)
+    keys[0:BLK, :] = k_ref[...]
+    values[0:BLK, :DH] = v_ref[...]
     values[:, DH:] = jnp.ones((NY * BLK, DH), BF16)
-    outs, sums = [], []
-    for g in range(KV_HEADS_HERE):
-        lanes = slice(g * DH, (g + 1) * DH)
-        keys[0:BLK, :] = k_ref[:, lanes]
-        values[0:BLK, :DH] = v_ref[:, lanes]
-        for i, message in enumerate((m1, m2, m3)):
-            rows = slice((i + 1) * BLK, (i + 2) * BLK)
-            keys[rows, :] = message[0:BLK, lanes]
-            values[rows, :DH] = message[BLK : 2 * BLK, lanes]
-        queries = arrived[:, 8 * g : 8 * g + 8, :].reshape(ROWS * GROUP, DH).astype(BF16)
-        parts, logs = [], []
-        for r in range(0, ROWS * GROUP, chunk):
-            s = dot_keys(queries[r : r + chunk], keys[...])
-            pieces = [
-                jnp.where(columns < limits[b][r : r + chunk], s[:, b * BLK : (b + 1) * BLK], HIDDEN) for b in range(NY)
-            ]
-            top = jnp.max(functools.reduce(jnp.maximum, pieces), axis=1, keepdims=True)
-            top = jnp.maximum(top, FLOOR)
-            probs = jnp.concatenate([jnp.exp2((p - top) * EXPONENT).astype(BF16) for p in pieces], axis=1)
-            acc = dot_values(probs, values[...])
-            total = acc[:, DH:]
-            some = total > 0.0
-            parts.append(acc[:, :DH] / jnp.where(some, total, 1.0))
-            logs.append(jnp.where(some, top * EXPONENT + jnp.log2(jnp.where(some, total, 1.0)), HIDDEN))
-        outs.append(jnp.concatenate(parts, axis=0).reshape(ROWS, GROUP, DH))
-        sums.append(jnp.concatenate(logs, axis=0))
-    lane = lax.broadcasted_iota(jnp.int32, (ROWS * GROUP, DH), 1)
-    log = jnp.where(lane < 64, sums[0], sums[1])
+    for i, message in enumerate((m1, m2)):
+        rows = slice((i + 1) * BLK, (i + 2) * BLK)
+        keys[rows, :] = message[0:BLK, :]
+        values[rows, :DH] = message[BLK + 16 :, :]
+    keys[3 * BLK :, :] = k3[0:BLK, :]
+    values[3 * BLK :, :DH] = v3[...]
+    queries = jnp.where(g == 0, arrived[:, :GROUP, :], arrived[:, GROUP : 2 * GROUP, :])
+    queries = queries.reshape(ROWS * GROUP, DH).astype(BF16)
+    starts = range(0, ROWS * GROUP, chunk)
+    parts, logs = [], []
+    s = dot_keys(queries[0:chunk], keys[...])
+    for r in starts:
+        following = dot_keys(queries[r + chunk : r + 2 * chunk], keys[...]) if r + chunk < ROWS * GROUP else None
+        pieces = [
+            jnp.where(columns < limits[b][r : r + chunk], s[:, b * BLK : (b + 1) * BLK], HIDDEN) for b in range(NY)
+        ]
+        top = jnp.max(functools.reduce(jnp.maximum, pieces), axis=1, keepdims=True)
+        top = jnp.maximum(top, FLOOR)
+        probs = jnp.concatenate([jnp.exp2((p - top) * EXPONENT).astype(BF16) for p in pieces], axis=1)
+        acc = dot_values(probs, values[...])
+        total = acc[:, DH:]
+        some = total > 0.0
+        parts.append(acc[:, :DH] / jnp.where(some, total, 1.0))
+        logs.append(jnp.where(some, top * EXPONENT + jnp.log2(jnp.where(some, total, 1.0)), HIDDEN))
+        s = following
+    out = jnp.concatenate(parts, axis=0).reshape(ROWS, GROUP, DH)
+    log = jnp.concatenate(logs, axis=0)
+    lane = lax.broadcasted_iota(jnp.int32, (ROWS * GROUP, DH), 1) & 63
     high = log.astype(BF16).astype(F32)
     middle = (log - high).astype(BF16).astype(F32)
     low = log - high - middle
-    lane = lane & 63
     log = jnp.where(lane == 0, high, jnp.where(lane == 1, middle, low)).reshape(ROWS, GROUP, DH)
-    o_ref[...] = jnp.concatenate(outs + [log], axis=1).astype(BF16)
-
-
-def rows_attention(valid, msg, k, v, others, chunk=128):
-    whole = pl.BlockSpec(memory_space=pltpu.VMEM)
+
+    @pl.when(g == 0)
+    def _():
+        sent[:, 0:8, :] = out
+        sent[:, 8:16, :] = log
+
+    @pl.when(g == 1)
+    def _():
+        both = jnp.where(lane.reshape(ROWS, GROUP, DH) == lax.broadcasted_iota(jnp.int32, log.shape, 2), sent[:, 8:16, :], log)
+        o_ref[...] = jnp.concatenate([sent[:, 0:8, :], out, both], axis=1).astype(BF16)
+
+
+def rows_attention(valid, msg, k, v, others, after, chunk=128):
+    whole = pl.BlockSpec(msg.shape, lambda g: (0, 0, 0))
+    block = pl.BlockSpec((BLK, DH), lambda g: (0, g))
+    other = [pl.BlockSpec((array.shape[0], DH), lambda g: (0, g)) for array in others]
+    unread = [pl.BlockSpec(memory_space=pl.ANY)] * len(after)
     return pl.pallas_call(
         functools.partial(rows_kernel, chunk),
-        in_specs=[pl.BlockSpec(memory_space=pltpu.SMEM)] + [whole] * 6,
+        grid=(KV_HEADS_HERE,),
+        in_specs=[pl.BlockSpec(memory_space=pltpu.SMEM), whole, block, block, *other, *unread],
         out_specs=whole,
-        scratch_shapes=[pltpu.VMEM((NY * BLK, DH), BF16), pltpu.VMEM((NY * BLK, 2 * DH), BF16)],
+        scratch_shapes=[
+            pltpu.VMEM((NY * BLK, DH), BF16),
+            pltpu.VMEM((NY * BLK, 2 * DH), BF16),
+            pltpu.VMEM((ROWS, 2 * GROUP, DH), F32),
+        ],
         out_shape=jax.ShapeDtypeStruct(msg.shape, BF16),
-        compiler_params=pltpu.CompilerParams(vmem_limit_bytes=40 << 20),
-        cost_estimate=pl.CostEstimate(flops=1_100_000_000, bytes_accessed=3 << 20, transcendentals=2 << 20),
+        compiler_params=pltpu.CompilerParams(vmem_limit_bytes=20 << 20),
+        cost_estimate=pl.CostEstimate(flops=7_000_000_000, bytes_accessed=3 << 20, transcendentals=2 << 20),
         name="rows_attention",
-    )(valid, msg, k, v, *others)
+    )(valid, msg, k, v, *others, *after)
 
 
 def merge_kernel(msg_ref, o_ref):
@@ -173,8 +197,9 @@
             factor = jnp.exp2(log - jnp.max(log, axis=0, keepdims=True))
             total = jnp.sum(factor, axis=0)
             merged = jnp.sum(factor * arrived[:, h, 8 * g : 8 * g + 8, :], axis=0) / total
-            start = (h * KV_HEADS_HERE + g) * GROUP
-            o_ref[start : start + GROUP, :] = merged
+            for i in range(GROUP):
+                at = ((h * KV_HEADS_HERE + g) * GROUP + i) * DH
+                o_ref[0:1, at : at + DH] = merged[i : i + 1].astype(BF16)
 
 
 def merge(msg):
@@ -183,7 +208,8 @@
         merge_kernel,
         in_specs=[whole],
         out_specs=whole,
-        out_shape=jax.ShapeDtypeStruct((NXL * NCORE * KV_HEADS_HERE * GROUP, DH), F32),
+        out_shape=jax.ShapeDtypeStruct((1, NXL * NCORE * KV_HEADS_HERE * GROUP * DH), BF16),
+        compiler_params=pltpu.CompilerParams(vmem_limit_bytes=6 << 20),
         name="merge",
     )(msg)
 
@@ -197,6 +223,36 @@
     return high.astype(BF16), (number - high * 256).astype(BF16)
 
 
+def message_kernel(offset_ref, q_ref, _, o_ref, rows):
+    offset = offset_ref[0]
+    high, low = (offset >> 8).astype(F32), (offset & 255).astype(F32)
+    lane = lax.broadcasted_iota(jnp.int32, (GROUP, DH), 1)
+    limit = jnp.where(lane < 64, high, low)
+    heads = KV_HEADS_HERE * GROUP
+    for h in range(NXL * NCORE):
+        for i in range(heads):
+            at = (h * heads + i) * DH
+            rows[h, i : i + 1, :] = q_ref[0:1, at : at + DH].astype(F32)
+        rows[h, heads:, :] = limit
+    o_ref[...] = jnp.broadcast_to(rows[...].astype(BF16)[None], o_ref.shape)
+
+
+def row_message(offsets, query_rows, after):
+    whole = pl.BlockSpec(memory_space=pltpu.VMEM)
+    groups = NXL * NCORE
+    out = pl.pallas_call(
+        message_kernel,
+        in_specs=[pl.BlockSpec(memory_space=pltpu.SMEM), whole, pl.BlockSpec(memory_space=pl.ANY)],
+        out_specs=whole,
+        scratch_shapes=[pltpu.VMEM((groups, 24, DH), F32)],
+        out_shape=jax.ShapeDtypeStruct((NZ * NXH, groups, 24, DH), BF16),
+        compiler_params=pltpu.CompilerParams(vmem_limit_bytes=6 << 20),
+        cost_estimate=pl.CostEstimate(flops=10**12, bytes_accessed=1 << 20, transcendentals=0),
+        name="row_message",
+    )(offsets, query_rows, after)
+    return out.reshape(PEERS, 24, DH)
+
+
 def place(z, xh):
     return (z % NZ) * NXH + xh
 
@@ -205,41 +261,84 @@
     return [lax.ppermute(array, "y", shift(NY, by)) for by in (1, -1, 2)]
 
 
-def spread_anchor(kv):
-    quarters = [jnp.concatenate([kv[r : r + QUARTER], kv[BLK + r : BLK + r + QUARTER]]) for r in range(0, BLK, QUARTER)]
+def ring_blocks(kv):
+    before, behind = lax.ppermute(kv, "y", shift(NY, 1)), lax.ppermute(kv, "y", shift(NY, -1))
+    keys, values = halves(before, behind)
+    far_keys = lax.ppermute(keys, "y", shift(NY, 1))
+    far_values = lax.ppermute(values, "y", shift(NY, -1))
+    return [before, behind, far_keys, far_values], keys
+
+
+def anchor_quarters(k, v):
+    quarters = [jnp.concatenate([k[r : r + QUARTER], v[r : r + QUARTER]]) for r in range(0, BLK, QUARTER)]
     current = jnp.where(lax.axis_index(CTX) == 0, quarters[0], jnp.zeros_like(quarters[0]))
     for y in range(1, NY):
         current = current + lax.ppermute(quarters[y], CTX, [(0, y)])
+    return current
+
+
+def anchor_tree(current, after):
     sent = [lax.ppermute(current, ZX, [(0, place(z, 0))]) for z in (2, 4, 6)]
-    current = current + sent[0] + sent[1] + sent[2]
+    current = join([current] + sent, (after,))
     even = (0, 2, 4, 6)
     sent = [
         lax.ppermute(current, ZX, [(place(z, 0), place(z + dz, xh)) for z in even]) for dz, xh in ((0, 1), (1, 0), (1, 1))
     ]
-    current = current + sent[0] + sent[1] + sent[2]
-    return [current] + to_ring(current)
+    return current + sent[0] + sent[1] + sent[2]
+
+
+def join_kernel(count, *refs):
+    total = refs[0][...]
+    for ref in refs[1:count]:
+        total = total + ref[...]
+    refs[-1][...] = total
+
+
+def join(parts, after=()):
+    whole = pl.BlockSpec(memory_space=pltpu.VMEM)
+    return pl.pallas_call(
+        functools.partial(join_kernel, len(parts)),
+        in_specs=[whole] * len(parts) + [pl.BlockSpec(memory_space=pl.ANY)] * len(after),
+        out_specs=whole,
+        out_shape=jax.ShapeDtypeStruct(parts[0].shape, BF16),
+        compiler_params=SMALL,
+        cost_estimate=LONG,
+        name="join",
+    )(*parts, *after)
+
+
+def halves_kernel(before, behind, keys, values):
+    keys[...] = before[0 : BLK + 16, :]
+    values[...] = behind[BLK + 16 :, :]
+
+
+def halves(before, behind):
+    whole = pl.BlockSpec(memory_space=pltpu.VMEM)
+    return pl.pallas_call(
+        halves_kernel,
+        in_specs=[whole] * 2,
+        out_specs=[whole] * 2,
+        out_shape=[jax.ShapeDtypeStruct((rows, before.shape[1]), BF16) for rows in (BLK + 16, BLK)],
+        compiler_params=SMALL,
+        cost_estimate=LONG,
+        name="halves",
+    )(before, behind)
 
 
 def on_device(ctx_query, ctx_key, ctx_value, valid, query_rows, offsets):
     high, low = digits_of(valid)
-    extra = jnp.concatenate([jnp.broadcast_to(high[None], (16, DH)), jnp.broadcast_to(low[None], (16, DH))], axis=1)
-    kv = jnp.concatenate([ctx_key, ctx_value, extra], axis=0)
-    others = to_ring(kv)
-
-    high, low = digits_of(offsets)
-    limit = jnp.concatenate(
-        [jnp.broadcast_to(high[None, None], (4, 8, 64)), jnp.broadcast_to(low[None, None], (4, 8, 64))], axis=2
-    )
-    message = jnp.concatenate([query_rows.reshape(4, 16, DH), limit], axis=1)
-    message = jnp.broadcast_to(message[None], (NZ * NXH, 4, 24, DH)).reshape(PEERS, 24, DH)
+    extra = jnp.concatenate([jnp.broadcast_to(high[None], (8, 2 * DH)), jnp.broadcast_to(low[None], (8, 2 * DH))], axis=0)
+    kv = jnp.concatenate([ctx_key, extra, ctx_value], axis=0)
+    current = anchor_quarters(ctx_key, ctx_value)
+    others, keys = ring_blocks(kv)
+    message = row_message(offsets, query_rows, current)
     message = lax.all_to_all(message, PLANE, 0, 0, tiled=True)
-
-    pieces = spread_anchor(kv)
-    partial = rows_attention(valid, message, ctx_key, ctx_value, others)
+    current = anchor_tree(current, keys)
+    pieces = [current] + to_ring(current)
+    partial = rows_attention(valid, message, ctx_key, ctx_value, others, [current])
     partial = lax.all_to_all(partial, PLANE, 0, 0, tiled=True)
     block_out = block_attention(valid, ctx_query, ctx_key, ctx_value, pieces)
-    query_out = merge(partial).astype(BF16).reshape(1, -1)
-    return (block_out, query_out)
+    return (block_out, merge(partial))
 
 
 def solution(mesh):

time: 97.6 us -> 82.9 us (0.85)
  waiting for transfers between devices: 21.1 us -> 6.77 us
  local copies, waits for them, and re-layouts: 5.95 us -> 1.28 us
  Pallas kernels: 17 us -> 21.3 us
  other arithmetic: 5.26 us -> 1.93 us
  starting transfers between devices: 45.3 us -> 48.4 us
    ppermute x9 -> x13, waiting for transfers between devices: 15.1 us -> 2.65 us  [the longest x3 1.6 us: anchor_tree(): lax.ppermute(current, ZX, [(place(z, 0), place(z + dz, xh)) for z in even])]
    ppermute x9 -> x13, starting transfers between devices: 18.4 us -> 29.4 us  [the longest x3 8.37 us: anchor_tree(): lax.ppermute(current, ZX, [(place(z, 0), place(z + dz, xh)) for z in even])]
    all_to_all x1, starting transfers between devices: 13 us -> 6.27 us  [on_device(): message = lax.all_to_all(message, PLANE, 0, 0, tiled=True)]
    ppermute x6 -> x3, waiting for transfers between devices: 6.01 us -> 0.01 us  [to_ring(): return [lax.ppermute(array, 'y', shift(NY, by)) for by in (1, -1, 2)]]
    unnamed x17 -> x12, local copies, waits for them, and re-layouts: 5.09 us -> 0.04 us
    pallas_call x1 -> x4, Pallas kernels: 4.54 us -> 9.26 us  [the longest x1 6.02 us: rows_attention(): pl.pallas_call(functools.partial(rows_kernel, chunk), grid=(KV_HEADS_HERE...]
    all_to_all x1, waiting for transfers between devices: 0.01 us -> 4.11 us  [on_device(): partial = lax.all_to_all(partial, PLANE, 0, 0, tiled=True)]
    ppermute x6 -> x3, starting transfers between devices: 5.69 us -> 3.25 us  [to_ring(): return [lax.ppermute(array, 'y', shift(NY, by)) for by in (1, -1, 2)]]
  transfers between devices with their start and end apart: 17 -> 18, of which waited for: 5 -> 3; matrix products, arithmetic and copies ran while one was open for 4% -> 2% of each run, Pallas kernels for 15% -> 25%
where the time goes in v2:
time: 82.9 us; the launch traced here: 82 us
  starting transfers between devices  48.4 us (58%)
  Pallas kernels  21.3 us (26%)
  waiting for transfers between devices  6.77 us (8%)
  between operations  2.24 us (3%)
  other arithmetic  1.93 us (2%)
  local copies, waits for them, and re-layouts  1.28 us (2%)
    pallas_call x1, Pallas kernels, block_attention(): pl.pallas_call(functools.partial(block_kernel, heads, chunk, stack), grid...  10.9 us
    all_to_all x1, starting transfers between devices, on_device(): partial = lax.all_to_all(partial, PLANE, 0, 0, tiled=True)  9.51 us
    ppermute x3, starting transfers between devices, anchor_tree(): lax.ppermute(current, ZX, [(place(z, 0), place(z + dz, xh)) for z in even])  8.37 us
    ppermute x3, starting transfers between devices, anchor_tree(): sent = [lax.ppermute(current, ZX, [(0, place(z, 0))]) for z in (2, 4, 6)]  7.96 us
    ppermute x3, starting transfers between devices, anchor_quarters(): current = current + lax.ppermute(quarters[y], CTX, [(0, y)])  7.62 us
    all_to_all x1, starting transfers between devices, on_device(): message = lax.all_to_all(message, PLANE, 0, 0, tiled=True)  6.27 us
    pallas_call x1, Pallas kernels, rows_attention(): pl.pallas_call(functools.partial(rows_kernel, chunk), grid=(KV_HEADS_HERE...  6.02 us
    all_to_all x1, waiting for transfers between devices, on_device(): partial = lax.all_to_all(partial, PLANE, 0, 0, tiled=True)  4.11 us
  transfers between devices with their start and end apart: 18, of which 3 were waited for; matrix products, arithmetic and copies ran while one was open for 2% of the time, Pallas kernels for 25%

profile of v2, /device:TPU:1, one launch (start us, length us, event | category | flops | bytes accessed | tf_op | source)
XLA Modules:
  0.0 82.0 jit_solution(1077563747394525431)
XLA Ops:
  0.6 0.0 copy-start
  0.6 0.0 copy-start.2
  0.7 1.2 %fusion.3 = (bf16[128,256]{1,0:T(8,128)(2,1)S(1)}, bf16[128,256]{1,0:T(8,128)(2,1)S(1)}, bf16[128,256]{1,0:T(8,128)(2,1)S(1)}, bf16[128,256]{1,0:T(8,128)(2,1)S(...) fusion(bf16[512,256]{1,0:T(8,128)(2,1)} %k_ref.3, ...), kind=kLoop, calls=%fused_computation.9 | loop fusion | bytes 1048576 | tf_op jit(solution)/shard_map/slice | solution.py:273
  1.8 4.0 %collective-permute-start = (bf16[256,256]{1,0:T(8,128)(2,1)S(1)}, bf16[256,256]{1,0:T(8,128)(2,1)S(1)}, u32[]{:S(2)}, u32[]{:S(2)}) collective-permute-start(bf16[256,256]{1,0:T(8,128)(2,1)S(1)} %pad_maximum_fusion.1), channel_id=1, source_target_pairs={{0,4},{1,5},{2,6},{3,7}} | collective-permute-start | bytes 393224 | tf_op jit(solution)/shard_map/ppermute | solution.py:276
  5.9 0.0 copy-start.5
  5.9 2.3 %collective-permute-start.1 = (bf16[256,256]{1,0:T(8,128)(2,1)S(1)}, bf16[256,256]{1,0:T(8,128)(2,1)S(1)}, u32[]{:S(2)}, u32[]{:S(2)}) collective-permute-start(bf16[256,256]{1,0:T(8,128)(2,1)S(1)} %pad_maximum_fusion.2), channel_id=1, source_target_pairs={{0,8},{1,9},{2,10},{3,11}} | collective-permute-start | bytes 393224 | tf_op jit(solution)/shard_map/ppermute | solution.py:276
  8.2 1.3 %collective-permute-start.2 = (bf16[256,256]{1,0:T(8,128)(2,1)S(1)}, bf16[256,256]{1,0:T(8,128)(2,1)S(1)}, u32[]{:S(2)}, u32[]{:S(2)}) collective-permute-start(bf16[256,256]{1,0:T(8,128)(2,1)S(1)} %pad_maximum_fusion.3), channel_id=1, source_target_pairs={{0,12},{1,13},{2,14},{3,15}} | collective-permute-start | bytes 393224 | tf_op jit(solution)/shard_map/ppermute | solution.py:276
  10.2 0.1 pad.2.clone
  10.3 1.1 %pad_maximum_fusion = bf16[1040,256]{1,0:T(8,128)(2,1)} fusion(bf16[512,256]{1,0:T(8,128)(2,1)S(1)} %copy-done.2, bf16[512,256]{1,0:T(8,128)(2,1)S(1)} %copy-done, bf16[1040]{0:T(1024)(128)(2,1)S(1)} %pad.2.clone, bf16[1040]{0:T(1024)(128)(2,1)S(1)} %pad.1.clone), kind=kLoop, calls=%fused_computation | loop fusion | flops 2129920 | bytes 1060928 | tf_op jit(solution)/shard_map/concatenate | solution.py:331
  11.5 0.0 collective-permute-start.6
  11.5 2.7 %collective-permute-start.7 = (bf16[1040,256]{1,0:T(8,128)(2,1)}, bf16[1040,256]{1,0:T(8,128)(2,1)}, u32[]{:S(2)}, u32[]{:S(2)}) collective-permute-start(bf16[1040,256]{1,0:T(8,128)(2,1)} %pad_maximum_fusion), channel_id=1, source_target_pairs={{0,12},{4,0},{8,4},{12,8},{1,13},{5,1},{9,5},{13,9},{2,14},{6,2},{... | collective-permute-start | bytes 1597448 | tf_op jit(solution)/shard_map/ppermute | solution.py:265
  14.8 0.0 collective-permute-done
  14.8 0.0 collective-permute-done.1
  14.8 0.0 collective-permute-done.2
  14.8 0.7 fusion.2.refs_0_._
  15.6 1.9 %collective-permute-start.3 = (bf16[256,256]{1,0:T(8,128)(2,1)}, bf16[256,256]{1,0:T(8,128)(2,1)}, u32[]{:S(2)}, u32[]{:S(2)}) collective-permute-start(bf16[256,256]{1,0:T(8,128)(2,1)} %fusion.2.refs_0_._), channel_id=1, source_target_pairs={{0,64},{1,65},{2,66},{3,67},{4,68},{5,69},{6,70},{7,71},{8,72},{9,... | collective-permute-start | bytes 393224 | tf_op jit(solution)/shard_map/ppermute | solution.py:281
  17.5 4.1 %collective-permute-start.4 = (bf16[256,256]{1,0:T(8,128)(2,1)}, bf16[256,256]{1,0:T(8,128)(2,1)}, u32[]{:S(2)}, u32[]{:S(2)}) collective-permute-start(bf16[256,256]{1,0:T(8,128)(2,1)} %fusion.2.refs_0_._), channel_id=1, source_target_pairs={{0,128},{1,129},{2,130},{3,131},{4,132},{5,133},{6,134},{7,135},{8... | collective-permute-start | bytes 393224 | tf_op jit(solution)/shard_map/ppermute | solution.py:281
  21.6 1.9 %collective-permute-start.5 = (bf16[256,256]{1,0:T(8,128)(2,1)}, bf16[256,256]{1,0:T(8,128)(2,1)}, u32[]{:S(2)}, u32[]{:S(2)}) collective-permute-start(bf16[256,256]{1,0:T(8,128)(2,1)} %fusion.2.refs_0_._), channel_id=1, source_target_pairs={{0,192},{1,193},{2,194},{3,195},{4,196},{5,197},{6,198},{7,199},{8... | collective-permute-start | bytes 393224 | tf_op jit(solution)/shard_map/ppermute | solution.py:281
  23.5 0.8 row_message.1
  24.3 6.3 %all-to-all-start = ((bf16[64,24,128]{2,1,0:T(8,128)(2,1)}), bf16[64,24,128]{2,1,0:T(8,128)(2,1)}, u32[]{:S(2)}, u32[]{:S(2)}) async-start(bf16[64,24,128]{2,1,0:T(8,128)(2,1)} %bitcast.2), calls=%async_computation | async-start | bytes 786432 | tf_op jit(solution)/shard_map/all_to_all | solution.py:335
  30.6 0.0 collective-permute-done.6.before.m1
  30.6 0.0 collective-permute-done.7.behind.m2
  30.6 1.2 %halves.1 = (bf16[528,256]{1,0:T(8,128)(2,1)S(1)}, bf16[512,256]{1,0:T(8,128)(2,1)S(1)}) custom-call(bf16[1040,256]{1,0:T(8,128)(2,1)} %collective-permute-done.6.before.m1, bf16[1040,256]{1,0:T(8,128)(2,1)} %collective-permute-done.7.behind.m2), custom_call_target="tpu_custom_call" | custom-call | flops 999999995904 | bytes 1048576 | tf_op jit(solution)/shard_map/halves/pallas_call | solution.py:317
  31.9 0.0 collective-permute-done.3.refs_1_
  31.9 0.0 collective-permute-done.4.refs_2_
  31.9 0.0 copy-start.1
  31.9 0.0 copy-start.3
  31.9 1.2 %join.1 = bf16[256,256]{1,0:T(8,128)(2,1)S(1)} custom-call(bf16[256,256]{1,0:T(8,128)(2,1)} %fusion.2.refs_0_._, bf16[256,256]{1,0:T(8,128)(2,1)} %collective-permute-done.3.refs_1_, bf16[256,256]{1,0:T(8,128)(2,1)} %collective-permute-done.4.refs_2_, bf16[256,256]{1,0:T(8,128)(2,1)} %collective-permute-done.5.refs_3_, ...), custom_call_target="tpu_custom_call" | custom-call | flops 999999995904 | bytes 1048576 | tf_op jit(solution)/shard_map/join/pallas_call | solution.py:299
  33.1 5.8 %collective-permute-start.10 = (bf16[256,256]{1,0:T(8,128)(2,1)S(1)}, bf16[256,256]{1,0:T(8,128)(2,1)S(1)}, u32[]{:S(2)}, u32[]{:S(2)}) collective-permute-start(bf16[256,256]{1,0:T(8,128)(2,1)S(1)} %join.1), channel_id=1, source_target_pairs={{0,48},{64,112},{128,176},{192,240},{1,49},{65,113},{129,177},{193... | collective-permute-start | bytes 393224 | tf_op jit(solution)/shard_map/ppermute | solution.py:285
  38.9 1.3 %collective-permute-start.8 = (bf16[256,256]{1,0:T(8,128)(2,1)S(1)}, bf16[256,256]{1,0:T(8,128)(2,1)S(1)}, u32[]{:S(2)}, u32[]{:S(2)}) collective-permute-start(bf16[256,256]{1,0:T(8,128)(2,1)S(1)} %join.1), channel_id=1, source_target_pairs={{0,16},{64,80},{128,144},{192,208},{1,17},{65,81},{129,145},{193,2... | collective-permute-start | bytes 393224 | tf_op jit(solution)/shard_map/ppermute | solution.py:285
  40.2 1.3 %collective-permute-start.9 = (bf16[256,256]{1,0:T(8,128)(2,1)S(1)}, bf16[256,256]{1,0:T(8,128)(2,1)S(1)}, u32[]{:S(2)}, u32[]{:S(2)}) collective-permute-start(bf16[256,256]{1,0:T(8,128)(2,1)S(1)} %join.1), channel_id=1, source_target_pairs={{0,32},{64,96},{128,160},{192,224},{1,33},{65,97},{129,161},{193,2... | collective-permute-start | bytes 393224 | tf_op jit(solution)/shard_map/ppermute | solution.py:285
  41.5 0.2 collective-permute-start.14
  41.7 2.6 %collective-permute-start.15 = (bf16[512,256]{1,0:T(8,128)(2,1)S(1)}, bf16[512,256]{1,0:T(8,128)(2,1)S(1)}, u32[]{:S(2)}, u32[]{:S(2)}) collective-permute-start(bf16[512,256]{1,0:T(8,128)(2,1)S(1)} %get-tuple-element.5), channel_id=1, source_target_pairs={{0,12},{4,0},{8,4},{12,8},{1,13},{5,1},{9,5},{13,9},{2,14},{6,2},{... | collective-permute-start | bytes 786440 | tf_op jit(solution)/shard_map/ppermute | solution.py:268
  44.3 1.6 %collective-permute-done.9 = bf16[256,256]{1,0:T(8,128)(2,1)S(1)} collective-permute-done((bf16[256,256]{1,0:T(8,128)(2,1)S(1)}, bf16[256,256]{1,0:T(8,128)(2,1)S(1)}, u32[]{:S(2)}, u32[]{:S(2)}) %collective-permute-start.9) | collective-permute-done | bytes 131104 | tf_op jit(solution)/shard_map/ppermute | solution.py:285
  45.9 0.0 copy-start.4
  45.9 0.2 collective-permute-start.11
  46.1 2.6 %collective-permute-start.12 = (bf16[256,256]{1,0:T(8,128)(2,1)S(1)}, bf16[256,256]{1,0:T(8,128)(2,1)}, u32[]{:S(2)}, u32[]{:S(2)}) collective-permute-start(bf16[256,256]{1,0:T(8,128)(2,1)S(1)} %add_add_fusion.a0.rest_0_), channel_id=1, source_target_pairs={{0,12},{4,0},{8,4},{12,8},{1,13},{5,1},{9,5},{13,9},{2,14},{6,2},{... | collective-permute-start | bytes 393224 | tf_op jit(solution)/shard_map/ppermute | solution.py:261
  48.7 0.5 collective-permute-start.13
  49.2 0.0 collective-permute-done.15.v3
  49.2 1.0 %collective-permute-done.14.k3 = bf16[528,256]{1,0:T(8,128)(2,1)S(1)} collective-permute-done((bf16[528,256]{1,0:T(8,128)(2,1)S(1)}, bf16[528,256]{1,0:T(8,128)(2,1)S(1)}, u32[]{:S(2)}, u32[]{:S(2)}) %collective-permute-start.14) | collective-permute-done | bytes 270368 | tf_op jit(solution)/shard_map/ppermute | solution.py:267
  50.2 0.0 all-to-all-done.msg_ref
  50.2 6.0 %rows_attention.1 = bf16[64,24,128]{2,1,0:T(8,128)(2,1)} custom-call(s32[1]{0:T(128)S(6)} %copy.8.valid_ref, bf16[64,24,128]{2,1,0:T(8,128)(2,1)} %all-to-all-done.msg_ref, bf16[512,256]{1,0:T(8,128)(2,1)S(1)} %copy-done.1, bf16[512,256]{1,0:T(8,128)(2,1)S(1)} %copy-done.3, bf16[1040,256]{1,0:T(8,128)(2,1)} %collective-permute-done.6.before.m1, ...), custom_call_target="tpu_custom_call" | custom-call | flops 7000000000 | bytes 3145728 | tf_op jit(solution)/shard_map/rows_attention/pallas_call | solution.py:173
  56.2 9.5 %all-to-all-start.1 = ((bf16[64,24,128]{2,1,0:T(8,128)(2,1)}), bf16[64,24,128]{2,1,0:T(8,128)(2,1)S(1)}, u32[]{:S(2)}, u32[]{:S(2)}) async-start(bf16[64,24,128]{2,1,0:T(8,128)(2,1)} %rows_attention.1), calls=%async_computation.1 | async-start | bytes 786432 | tf_op jit(solution)/shard_map/all_to_all | solution.py:339
  65.8 0.0 collective-permute-done.12.a2
  65.8 0.0 collective-permute-done.13.a3
  65.8 10.9 %block_attention.1 = bf16[512,2048]{1,0:T(8,128)(2,1)} custom-call(s32[1]{0:T(128)S(6)} %copy.8.valid_ref, bf16[512,2048]{1,0:T(8,128)(2,1)S(1)} %copy-done.4, bf16[512,256]{1,0:T(8,128)(2,1)S(1)} %copy-done.1, bf16[512,256]{1,0:T(8,128)(2,1)S(1)} %copy-done.3, bf16[256,256]{1,0:T(8,128)(2,1)S(1)} %add_add_fusion.a0.rest_0_, ...), custom_call_target="tpu_custom_call" | custom-call | flops 12000000000 | bytes 5242880 | tf_op jit(solution)/shard_map/block_attention/pallas_call | solution.py:93
  76.7 4.1 %all-to-all-done.1.msg_ref = bf16[64,24,128]{2,1,0:T(8,128)(2,1)S(1)} async-done(((bf16[64,24,128]{2,1,0:T(8,128)(2,1)}), bf16[64,24,128]{2,1,0:T(8,128)(2,1)S(1)}, u32[]{:S(2)}, u32[]{:S(2)}) %all-to-all-start.1) | async-done | bytes 393248 | tf_op jit(solution)/shard_map/all_to_all | solution.py:339
  80.8 1.2 %merge.1 = bf16[1,8192]{1,0:T(2,128)(2,1)} custom-call(bf16[64,24,128]{2,1,0:T(8,128)(2,1)S(1)} %all-to-all-done.1.msg_ref), custom_call_target="tpu_custom_call" | custom-call | tf_op jit(solution)/shard_map/merge/pallas_call | solution.py:207
  (17 shorter events, 0.1 us)
Async XLA Ops:
  0.6 9.7 %copy-start = (bf16[512,256]{1,0:T(8,128)(2,1)S(1)}, bf16[512,256]{1,0:T(8,128)(2,1)}, u32[]{:S(2)}) copy-start(bf16[512,256]{1,0:T(8,128)(2,1)} %k_ref.3) | copy-start | bytes 786436
  0.6 9.7 %copy-start.2 = (bf16[512,256]{1,0:T(8,128)(2,1)S(1)}, bf16[512,256]{1,0:T(8,128)(2,1)}, u32[]{:S(2)}) copy-start(bf16[512,256]{1,0:T(8,128)(2,1)} %v_ref.3) | copy-start | bytes 786436
  1.8 13.0 %collective-permute-start = (bf16[256,256]{1,0:T(8,128)(2,1)S(1)}, bf16[256,256]{1,0:T(8,128)(2,1)S(1)}, u32[]{:S(2)}, u32[]{:S(2)}) collective-permute-start(bf16[256,256]{1,0:T(8,128)(2,1)S(1)} %pad_maximum_fusion.1), channel_id=1, source_target_pairs={{0,4},{1,5},{2,6},{3,7}} | collective-permute-start | bytes 393224 | tf_op jit(solution)/shard_map/ppermute | solution.py:276
  5.9 17.6 %copy-start.5 = (bf16[1,8192]{1,0:T(2,128)(2,1)S(1)}, bf16[1,8192]{1,0:T(2,128)(2,1)}, u32[]{:S(2)}) copy-start(bf16[1,8192]{1,0:T(2,128)(2,1)} %q_ref.3) | copy-start | bytes 49156
  5.9 8.9 %collective-permute-start.1 = (bf16[256,256]{1,0:T(8,128)(2,1)S(1)}, bf16[256,256]{1,0:T(8,128)(2,1)S(1)}, u32[]{:S(2)}, u32[]{:S(2)}) collective-permute-start(bf16[256,256]{1,0:T(8,128)(2,1)S(1)} %pad_maximum_fusion.2), channel_id=1, source_target_pairs={{0,8},{1,9},{2,10},{3,11}} | collective-permute-start | bytes 393224 | tf_op jit(solution)/shard_map/ppermute | solution.py:276
  8.2 6.6 %collective-permute-start.2 = (bf16[256,256]{1,0:T(8,128)(2,1)S(1)}, bf16[256,256]{1,0:T(8,128)(2,1)S(1)}, u32[]{:S(2)}, u32[]{:S(2)}) collective-permute-start(bf16[256,256]{1,0:T(8,128)(2,1)S(1)} %pad_maximum_fusion.3), channel_id=1, source_target_pairs={{0,12},{1,13},{2,14},{3,15}} | collective-permute-start | bytes 393224 | tf_op jit(solution)/shard_map/ppermute | solution.py:276
  11.5 19.2 %collective-permute-start.6 = (bf16[1040,256]{1,0:T(8,128)(2,1)}, bf16[1040,256]{1,0:T(8,128)(2,1)}, u32[]{:S(2)}, u32[]{:S(2)}) collective-permute-start(bf16[1040,256]{1,0:T(8,128)(2,1)} %pad_maximum_fusion), channel_id=1, source_target_pairs={{0,4},{4,8},{8,12},{12,0},{1,5},{5,9},{9,13},{13,1},{2,6},{6,10},{... | collective-permute-start | bytes 1597448 | tf_op jit(solution)/shard_map/ppermute | solution.py:265
  11.5 19.2 %collective-permute-start.7 = (bf16[1040,256]{1,0:T(8,128)(2,1)}, bf16[1040,256]{1,0:T(8,128)(2,1)}, u32[]{:S(2)}, u32[]{:S(2)}) collective-permute-start(bf16[1040,256]{1,0:T(8,128)(2,1)} %pad_maximum_fusion), channel_id=1, source_target_pairs={{0,12},{4,0},{8,4},{12,8},{1,13},{5,1},{9,5},{13,9},{2,14},{6,2},{... | collective-permute-start | bytes 1597448 | tf_op jit(solution)/shard_map/ppermute | solution.py:265
  15.6 16.3 %collective-permute-start.3 = (bf16[256,256]{1,0:T(8,128)(2,1)}, bf16[256,256]{1,0:T(8,128)(2,1)}, u32[]{:S(2)}, u32[]{:S(2)}) collective-permute-start(bf16[256,256]{1,0:T(8,128)(2,1)} %fusion.2.refs_0_._), channel_id=1, source_target_pairs={{0,64},{1,65},{2,66},{3,67},{4,68},{5,69},{6,70},{7,71},{8,72},{9,... | collective-permute-start | bytes 393224 | tf_op jit(solution)/shard_map/ppermute | solution.py:281
  17.5 14.4 %collective-permute-start.4 = (bf16[256,256]{1,0:T(8,128)(2,1)}, bf16[256,256]{1,0:T(8,128)(2,1)}, u32[]{:S(2)}, u32[]{:S(2)}) collective-permute-start(bf16[256,256]{1,0:T(8,128)(2,1)} %fusion.2.refs_0_._), channel_id=1, source_target_pairs={{0,128},{1,129},{2,130},{3,131},{4,132},{5,133},{6,134},{7,135},{8... | collective-permute-start | bytes 393224 | tf_op jit(solution)/shard_map/ppermute | solution.py:281
  21.6 10.3 %collective-permute-start.5 = (bf16[256,256]{1,0:T(8,128)(2,1)}, bf16[256,256]{1,0:T(8,128)(2,1)}, u32[]{:S(2)}, u32[]{:S(2)}) collective-permute-start(bf16[256,256]{1,0:T(8,128)(2,1)} %fusion.2.refs_0_._), channel_id=1, source_target_pairs={{0,192},{1,193},{2,194},{3,195},{4,196},{5,197},{6,198},{7,199},{8... | collective-permute-start | bytes 393224 | tf_op jit(solution)/shard_map/ppermute | solution.py:281
  24.3 25.9 %all-to-all-start = ((bf16[64,24,128]{2,1,0:T(8,128)(2,1)}), bf16[64,24,128]{2,1,0:T(8,128)(2,1)}, u32[]{:S(2)}, u32[]{:S(2)}) async-start(bf16[64,24,128]{2,1,0:T(8,128)(2,1)} %bitcast.2), calls=%async_computation | async-start | bytes 786432 | tf_op jit(solution)/shard_map/all_to_all | solution.py:335
  31.9 18.3 %copy-start.1 = (bf16[512,256]{1,0:T(8,128)(2,1)S(1)}, bf16[512,256]{1,0:T(8,128)(2,1)}, u32[]{:S(2)}) copy-start(bf16[512,256]{1,0:T(8,128)(2,1)} %k_ref.3) | copy-start | bytes 786436
  31.9 18.3 %copy-start.3 = (bf16[512,256]{1,0:T(8,128)(2,1)S(1)}, bf16[512,256]{1,0:T(8,128)(2,1)}, u32[]{:S(2)}) copy-start(bf16[512,256]{1,0:T(8,128)(2,1)} %v_ref.3) | copy-start | bytes 786436
  33.1 11.2 %collective-permute-start.10 = (bf16[256,256]{1,0:T(8,128)(2,1)S(1)}, bf16[256,256]{1,0:T(8,128)(2,1)S(1)}, u32[]{:S(2)}, u32[]{:S(2)}) collective-permute-start(bf16[256,256]{1,0:T(8,128)(2,1)S(1)} %join.1), channel_id=1, source_target_pairs={{0,48},{64,112},{128,176},{192,240},{1,49},{65,113},{129,177},{193... | collective-permute-start | bytes 393224 | tf_op jit(solution)/shard_map/ppermute | solution.py:285
  38.9 5.4 %collective-permute-start.8 = (bf16[256,256]{1,0:T(8,128)(2,1)S(1)}, bf16[256,256]{1,0:T(8,128)(2,1)S(1)}, u32[]{:S(2)}, u32[]{:S(2)}) collective-permute-start(bf16[256,256]{1,0:T(8,128)(2,1)S(1)} %join.1), channel_id=1, source_target_pairs={{0,16},{64,80},{128,144},{192,208},{1,17},{65,81},{129,145},{193,2... | collective-permute-start | bytes 393224 | tf_op jit(solution)/shard_map/ppermute | solution.py:285
  40.2 5.7 %collective-permute-start.9 = (bf16[256,256]{1,0:T(8,128)(2,1)S(1)}, bf16[256,256]{1,0:T(8,128)(2,1)S(1)}, u32[]{:S(2)}, u32[]{:S(2)}) collective-permute-start(bf16[256,256]{1,0:T(8,128)(2,1)S(1)} %join.1), channel_id=1, source_target_pairs={{0,32},{64,96},{128,160},{192,224},{1,33},{65,97},{129,161},{193,2... | collective-permute-start | bytes 393224 | tf_op jit(solution)/shard_map/ppermute | solution.py:285
  41.5 8.7 %collective-permute-start.14 = (bf16[528,256]{1,0:T(8,128)(2,1)S(1)}, bf16[528,256]{1,0:T(8,128)(2,1)S(1)}, u32[]{:S(2)}, u32[]{:S(2)}) collective-permute-start(bf16[528,256]{1,0:T(8,128)(2,1)S(1)} %get-tuple-element.4.refs_4_), channel_id=1, source_target_pairs={{0,4},{4,8},{8,12},{12,0},{1,5},{5,9},{9,13},{13,1},{2,6},{6,10},{... | collective-permute-start | bytes 811016 | tf_op jit(solution)/shard_map/ppermute | solution.py:267
  41.7 7.5 %collective-permute-start.15 = (bf16[512,256]{1,0:T(8,128)(2,1)S(1)}, bf16[512,256]{1,0:T(8,128)(2,1)S(1)}, u32[]{:S(2)}, u32[]{:S(2)}) collective-permute-start(bf16[512,256]{1,0:T(8,128)(2,1)S(1)} %get-tuple-element.5), channel_id=1, source_target_pairs={{0,12},{4,0},{8,4},{12,8},{1,13},{5,1},{9,5},{13,9},{2,14},{6,2},{... | collective-permute-start | bytes 786440 | tf_op jit(solution)/shard_map/ppermute | solution.py:268
  45.9 19.9 %copy-start.4 = (bf16[512,2048]{1,0:T(8,128)(2,1)S(1)}, bf16[512,2048]{1,0:T(8,128)(2,1)}, u32[]{:S(2)}) copy-start(bf16[512,2048]{1,0:T(8,128)(2,1)} %q_ref.2) | copy-start | bytes 6291460
  45.9 19.8 %collective-permute-start.11 = (bf16[256,256]{1,0:T(8,128)(2,1)S(1)}, bf16[256,256]{1,0:T(8,128)(2,1)S(1)}, u32[]{:S(2)}, u32[]{:S(2)}) collective-permute-start(bf16[256,256]{1,0:T(8,128)(2,1)S(1)} %add_add_fusion.a0.rest_0_), channel_id=1, source_target_pairs={{0,4},{4,8},{8,12},{12,0},{1,5},{5,9},{9,13},{13,1},{2,6},{6,10},{... | collective-permute-start | bytes 393224 | tf_op jit(solution)/shard_map/ppermute | solution.py:261
  46.1 19.7 %collective-permute-start.12 = (bf16[256,256]{1,0:T(8,128)(2,1)S(1)}, bf16[256,256]{1,0:T(8,128)(2,1)}, u32[]{:S(2)}, u32[]{:S(2)}) collective-permute-start(bf16[256,256]{1,0:T(8,128)(2,1)S(1)} %add_add_fusion.a0.rest_0_), channel_id=1, source_target_pairs={{0,12},{4,0},{8,4},{12,8},{1,13},{5,1},{9,5},{13,9},{2,14},{6,2},{... | collective-permute-start | bytes 393224 | tf_op jit(solution)/shard_map/ppermute | solution.py:261
  48.7 17.1 %collective-permute-start.13 = (bf16[256,256]{1,0:T(8,128)(2,1)S(1)}, bf16[256,256]{1,0:T(8,128)(2,1)}, u32[]{:S(2)}, u32[]{:S(2)}) collective-permute-start(bf16[256,256]{1,0:T(8,128)(2,1)S(1)} %add_add_fusion.a0.rest_0_), channel_id=1, source_target_pairs={{0,8},{4,12},{8,0},{12,4},{1,9},{5,13},{9,1},{13,5},{2,10},{6,14},... | collective-permute-start | bytes 393224 | tf_op jit(solution)/shard_map/ppermute | solution.py:261
  56.2 24.6 %all-to-all-start.1 = ((bf16[64,24,128]{2,1,0:T(8,128)(2,1)}), bf16[64,24,128]{2,1,0:T(8,128)(2,1)S(1)}, u32[]{:S(2)}, u32[]{:S(2)}) async-start(bf16[64,24,128]{2,1,0:T(8,128)(2,1)} %rows_attention.1), calls=%async_computation.1 | async-start | bytes 786432 | tf_op jit(solution)/shard_map/all_to_all | solution.py:339

commit v3 on v2

--- a/solution.py
+++ b/solution.py
@@ -28,7 +28,7 @@
 
 
 SMALL = pltpu.CompilerParams(vmem_limit_bytes=6 << 20)
-LONG = pl.CostEstimate(flops=10**12, bytes_accessed=1 << 20, transcendentals=0)
+LONG = pl.CostEstimate(flops=5 * 10**10, bytes_accessed=1 << 20, transcendentals=0)
 
 
 def dot_keys(queries, keys):
@@ -85,7 +85,7 @@
         s = following
 
 
-def block_attention(valid, q, k, v, pieces, heads=8, chunk=128, stack=2):
+def block_attention(valid, q, k, v, pieces, heads=8, chunk=128, stack=4):
     steps = GROUP // heads
     kv = pl.BlockSpec((BLK, DH), lambda g, i: (0, g))
     piece = pl.BlockSpec((2 * QUARTER, DH), lambda g, i: (0, g))
@@ -98,18 +98,18 @@
         scratch_shapes=[pltpu.VMEM((2 * BLK, DH), BF16), pltpu.VMEM((2 * BLK, 2 * DH), BF16)],
         out_shape=jax.ShapeDtypeStruct(q.shape, BF16),
         compiler_params=pltpu.CompilerParams(vmem_limit_bytes=20 << 20),
-        cost_estimate=pl.CostEstimate(flops=12_000_000_000, bytes_accessed=5 << 20, transcendentals=7 << 20),
+        cost_estimate=pl.CostEstimate(flops=10**9, bytes_accessed=5 << 20, transcendentals=7 << 20),
         name="block_attention",
     )(valid, q, k, v, *pieces)
 
 
-def rows_kernel(chunk, valid_ref, msg_ref, k_ref, v_ref, m1, m2, k3, v3, *rest):
+def rows_kernel(chunk, valid_ref, msg_ref, k_ref, v_ref, m1, m2, m3, *rest):
     o_ref, keys, values, sent = rest[-4:]
     g = pl.program_id(0)
     my_y = lax.axis_index("y")
     first = (lax.axis_index("z") * NXH + lax.axis_index("xh")) * NY
     valids, bases = [valid_ref[0].astype(F32)], [(first + my_y) * BLK]
-    for message, step in ((m1, 3), (m2, 1), (k3, 2)):
+    for message, step in ((m1, 3), (m2, 1), (m3, 2)):
         digits = message[BLK : BLK + 16, :].astype(F32)
         valids.append(digits[0:1, 0:1] * 256.0 + digits[8:9, 0:1])
         bases.append((first + lax.rem(my_y + step, NY)) * BLK)
@@ -121,12 +121,10 @@
     keys[0:BLK, :] = k_ref[...]
     values[0:BLK, :DH] = v_ref[...]
     values[:, DH:] = jnp.ones((NY * BLK, DH), BF16)
-    for i, message in enumerate((m1, m2)):
+    for i, message in enumerate((m1, m2, m3)):
         rows = slice((i + 1) * BLK, (i + 2) * BLK)
         keys[rows, :] = message[0:BLK, :]
         values[rows, :DH] = message[BLK + 16 :, :]
-    keys[3 * BLK :, :] = k3[0:BLK, :]
-    values[3 * BLK :, :DH] = v3[...]
     queries = jnp.where(g == 0, arrived[:, :GROUP, :], arrived[:, GROUP : 2 * GROUP, :])
     queries = queries.reshape(ROWS * GROUP, DH).astype(BF16)
     starts = range(0, ROWS * GROUP, chunk)
@@ -182,7 +180,7 @@
         ],
         out_shape=jax.ShapeDtypeStruct(msg.shape, BF16),
         compiler_params=pltpu.CompilerParams(vmem_limit_bytes=20 << 20),
-        cost_estimate=pl.CostEstimate(flops=7_000_000_000, bytes_accessed=3 << 20, transcendentals=2 << 20),
+        cost_estimate=pl.CostEstimate(flops=7 * 10**9, bytes_accessed=3 << 20, transcendentals=2 << 20),
         name="rows_attention",
     )(valid, msg, k, v, *others, *after)
 
@@ -247,7 +245,7 @@
         scratch_shapes=[pltpu.VMEM((groups, 24, DH), F32)],
         out_shape=jax.ShapeDtypeStruct((NZ * NXH, groups, 24, DH), BF16),
         compiler_params=pltpu.CompilerParams(vmem_limit_bytes=6 << 20),
-        cost_estimate=pl.CostEstimate(flops=10**12, bytes_accessed=1 << 20, transcendentals=0),
+        cost_estimate=pl.CostEstimate(flops=5 * 10**10, bytes_accessed=1 << 20, transcendentals=0),
         name="row_message",
     )(offsets, query_rows, after)
     return out.reshape(PEERS, 24, DH)
@@ -259,14 +257,6 @@
 
 def to_ring(array):
     return [lax.ppermute(array, "y", shift(NY, by)) for by in (1, -1, 2)]
-
-
-def ring_blocks(kv):
-    before, behind = lax.ppermute(kv, "y", shift(NY, 1)), lax.ppermute(kv, "y", shift(NY, -1))
-    keys, values = halves(before, behind)
-    far_keys = lax.ppermute(keys, "y", shift(NY, 1))
-    far_values = lax.ppermute(values, "y", shift(NY, -1))
-    return [before, behind, far_keys, far_values], keys
 
 
 def anchor_quarters(k, v):
@@ -279,12 +269,12 @@
 
 def anchor_tree(current, after):
     sent = [lax.ppermute(current, ZX, [(0, place(z, 0))]) for z in (2, 4, 6)]
-    current = join([current] + sent, (after,))
+    current = join([current] + sent, after)
     even = (0, 2, 4, 6)
     sent = [
         lax.ppermute(current, ZX, [(place(z, 0), place(z + dz, xh)) for z in even]) for dz, xh in ((0, 1), (1, 0), (1, 1))
     ]
-    return current + sent[0] + sent[1] + sent[2]
+    return current, sent
 
 
 def join_kernel(count, *refs):
@@ -307,35 +297,18 @@
     )(*parts, *after)
 
 
-def halves_kernel(before, behind, keys, values):
-    keys[...] = before[0 : BLK + 16, :]
-    values[...] = behind[BLK + 16 :, :]
-
-
-def halves(before, behind):
-    whole = pl.BlockSpec(memory_space=pltpu.VMEM)
-    return pl.pallas_call(
-        halves_kernel,
-        in_specs=[whole] * 2,
-        out_specs=[whole] * 2,
-        out_shape=[jax.ShapeDtypeStruct((rows, before.shape[1]), BF16) for rows in (BLK + 16, BLK)],
-        compiler_params=SMALL,
-        cost_estimate=LONG,
-        name="halves",
-    )(before, behind)
-
-
 def on_device(ctx_query, ctx_key, ctx_value, valid, query_rows, offsets):
     high, low = digits_of(valid)
     extra = jnp.concatenate([jnp.broadcast_to(high[None], (8, 2 * DH)), jnp.broadcast_to(low[None], (8, 2 * DH))], axis=0)
     kv = jnp.concatenate([ctx_key, extra, ctx_value], axis=0)
     current = anchor_quarters(ctx_key, ctx_value)
-    others, keys = ring_blocks(kv)
+    others = to_ring(kv)
     message = row_message(offsets, query_rows, current)
     message = lax.all_to_all(message, PLANE, 0, 0, tiled=True)
-    current = anchor_tree(current, keys)
+    near, sent = anchor_tree(current, others[:2])
+    partial = rows_attention(valid, message, ctx_key, ctx_value, others, [near])
+    current = join([near] + sent, (partial,))
     pieces = [current] + to_ring(current)
-    partial = rows_attention(valid, message, ctx_key, ctx_value, others, [current])
     partial = lax.all_to_all(partial, PLANE, 0, 0, tiled=True)
     block_out = block_attention(valid, ctx_query, ctx_key, ctx_value, pieces)
     return (block_out, merge(partial))

time: 82.9 us -> 79.4 us (0.958)
  Pallas kernels: 21.3 us -> 17.1 us
  waiting for transfers between devices: 6.77 us -> 10.4 us
  starting transfers between devices: 48.4 us -> 46.2 us
    ppermute x3 -> x6, waiting for transfers between devices: 0.01 us -> 9.77 us  [to_ring(): return [lax.ppermute(array, 'y', shift(NY, by)) for by in (1, -1, 2)]]
    ppermute x4 -> x0, starting transfers between devices: 5.43 us -> none  [the longest x1 2.67 us: ring_blocks(): lax.ppermute(kv, 'y', shift(NY, -1))]
    ppermute x3 -> x6, starting transfers between devices: 3.25 us -> 7.71 us  [to_ring(): return [lax.ppermute(array, 'y', shift(NY, by)) for by in (1, -1, 2)]]
    all_to_all x1, waiting for transfers between devices: 4.11 us -> 0.01 us  [on_device(): partial = lax.all_to_all(partial, PLANE, 0, 0, tiled=True)]
    ppermute x3, starting transfers between devices: 7.96 us -> 6.06 us  [anchor_tree(): sent = [lax.ppermute(current, ZX, [(0, place(z, 0))]) for z in (2, 4, 6)]]
    ppermute x3, waiting for transfers between devices: 1.6 us -> 0.01 us  [anchor_tree(): lax.ppermute(current, ZX, [(place(z, 0), place(z + dz, xh)) for z in even])]
    all_to_all x1, starting transfers between devices: 9.51 us -> 10.9 us  [on_device(): partial = lax.all_to_all(partial, PLANE, 0, 0, tiled=True)]
    pallas_call x1 -> x0, Pallas kernels: 1.24 us -> none  [halves(): pl.pallas_call(halves_kernel, in_specs=[whole] * 2, out_specs=[whole] * 2...]
  transfers between devices with their start and end apart: 18 -> 17, of which waited for: 3 -> 5; matrix products, arithmetic and copies ran while one was open for 2% -> 2% of each run, Pallas kernels for 25% -> 20%
where the time goes in v3:
time: 79.4 us; the launch traced here: 78.4 us
  starting transfers between devices  46.2 us (58%)
  Pallas kernels  17.1 us (22%)
  waiting for transfers between devices  10.4 us (13%)
  between operations  2.23 us (3%)
  local copies, waits for them, and re-layouts  1.27 us (2%)
  other arithmetic  1.26 us (2%)
    all_to_all x1, starting transfers between devices, on_device(): partial = lax.all_to_all(partial, PLANE, 0, 0, tiled=True)  10.9 us
    pallas_call x1, Pallas kernels, block_attention(): pl.pallas_call(functools.partial(block_kernel, heads, chunk, stack), grid...  9.93 us
    ppermute x6, waiting for transfers between devices, to_ring(): return [lax.ppermute(array, 'y', shift(NY, by)) for by in (1, -1, 2)]  9.77 us
    ppermute x3, starting transfers between devices, anchor_tree(): lax.ppermute(current, ZX, [(place(z, 0), place(z + dz, xh)) for z in even])  8.37 us
    ppermute x6, starting transfers between devices, to_ring(): return [lax.ppermute(array, 'y', shift(NY, by)) for by in (1, -1, 2)]  7.71 us
    ppermute x3, starting transfers between devices, anchor_quarters(): current = current + lax.ppermute(quarters[y], CTX, [(0, y)])  7.62 us
    ppermute x3, starting transfers between devices, anchor_tree(): sent = [lax.ppermute(current, ZX, [(0, place(z, 0))]) for z in (2, 4, 6)]  6.06 us
    all_to_all x1, starting transfers between devices, on_device(): message = lax.all_to_all(message, PLANE, 0, 0, tiled=True)  5.51 us
  transfers between devices with their start and end apart: 17, of which 5 were waited for; matrix products, arithmetic and copies ran while one was open for 2% of the time, Pallas kernels for 20%

profile of v3, /device:TPU:1, one launch (start us, length us, event | category | flops | bytes accessed | tf_op | source)
XLA Modules:
  0.0 78.4 jit_solution(7543489994535565349)
XLA Ops:
  0.6 0.0 copy-start
  0.6 0.0 copy-start.1
  0.6 1.2 %fusion.3 = (bf16[128,256]{1,0:T(8,128)(2,1)S(1)}, bf16[128,256]{1,0:T(8,128)(2,1)S(1)}, bf16[128,256]{1,0:T(8,128)(2,1)S(1)}, bf16[128,256]{1,0:T(8,128)(2,1)S(...) fusion(bf16[512,256]{1,0:T(8,128)(2,1)} %k_ref.3, ...), kind=kLoop, calls=%fused_computation.8 | loop fusion | bytes 1048576 | tf_op jit(solution)/shard_map/slice | solution.py:263
  1.8 4.0 %collective-permute-start = (bf16[256,256]{1,0:T(8,128)(2,1)S(1)}, bf16[256,256]{1,0:T(8,128)(2,1)S(1)}, u32[]{:S(2)}, u32[]{:S(2)}) collective-permute-start(bf16[256,256]{1,0:T(8,128)(2,1)S(1)} %pad_maximum_fusion.1), channel_id=1, source_target_pairs={{0,4},{1,5},{2,6},{3,7}} | collective-permute-start | bytes 393224 | tf_op jit(solution)/shard_map/ppermute | solution.py:266
  5.9 0.0 copy-start.3
  5.9 2.3 %collective-permute-start.1 = (bf16[256,256]{1,0:T(8,128)(2,1)S(1)}, bf16[256,256]{1,0:T(8,128)(2,1)S(1)}, u32[]{:S(2)}, u32[]{:S(2)}) collective-permute-start(bf16[256,256]{1,0:T(8,128)(2,1)S(1)} %pad_maximum_fusion.2), channel_id=1, source_target_pairs={{0,8},{1,9},{2,10},{3,11}} | collective-permute-start | bytes 393224 | tf_op jit(solution)/shard_map/ppermute | solution.py:266
  8.2 1.3 %collective-permute-start.2 = (bf16[256,256]{1,0:T(8,128)(2,1)S(1)}, bf16[256,256]{1,0:T(8,128)(2,1)S(1)}, u32[]{:S(2)}, u32[]{:S(2)}) collective-permute-start(bf16[256,256]{1,0:T(8,128)(2,1)S(1)} %pad_maximum_fusion.3), channel_id=1, source_target_pairs={{0,12},{1,13},{2,14},{3,15}} | collective-permute-start | bytes 393224 | tf_op jit(solution)/shard_map/ppermute | solution.py:266
  10.2 0.1 pad.2.clone
  10.3 0.0 copy-done
  10.3 1.1 %pad_maximum_fusion = bf16[1040,256]{1,0:T(8,128)(2,1)} fusion(bf16[512,256]{1,0:T(8,128)(2,1)S(1)} %copy-done.1, bf16[512,256]{1,0:T(8,128)(2,1)S(1)} %copy-done, bf16[1040]{0:T(1024)(128)(2,1)S(1)} %pad.2.clone, bf16[1040]{0:T(1024)(128)(2,1)S(1)} %pad.1.clone), kind=kLoop, calls=%fused_computation | loop fusion | flops 2129920 | bytes 1060928 | tf_op jit(solution)/shard_map/concatenate | solution.py:303
  11.5 0.0 collective-permute-start.6
  11.5 2.7 %collective-permute-start.7 = (bf16[1040,256]{1,0:T(8,128)(2,1)}, bf16[1040,256]{1,0:T(8,128)(2,1)S(1)}, u32[]{:S(2)}, u32[]{:S(2)}) collective-permute-start(bf16[1040,256]{1,0:T(8,128)(2,1)} %pad_maximum_fusion), channel_id=1, source_target_pairs={{0,12},{4,0},{8,4},{12,8},{1,13},{5,1},{9,5},{13,9},{2,14},{6,2},{... | collective-permute-start | bytes 1597448 | tf_op jit(solution)/shard_map/ppermute | solution.py:259
  14.8 0.0 collective-permute-done
  14.8 0.0 collective-permute-done.1
  14.8 0.0 collective-permute-done.2
  14.8 0.1 fusion.2.refs_0_._
  14.9 1.3 %collective-permute-start.3 = (bf16[256,256]{1,0:T(8,128)(2,1)S(1)}, bf16[256,256]{1,0:T(8,128)(2,1)S(1)}, u32[]{:S(2)}, u32[]{:S(2)}) collective-permute-start(bf16[256,256]{1,0:T(8,128)(2,1)S(1)} %fusion.2.refs_0_._), channel_id=1, source_target_pairs={{0,64},{1,65},{2,66},{3,67},{4,68},{5,69},{6,70},{7,71},{8,72},{9,... | collective-permute-start | bytes 393224 | tf_op jit(solution)/shard_map/ppermute | solution.py:271
  16.2 3.5 %collective-permute-start.4 = (bf16[256,256]{1,0:T(8,128)(2,1)S(1)}, bf16[256,256]{1,0:T(8,128)(2,1)S(1)}, u32[]{:S(2)}, u32[]{:S(2)}) collective-permute-start(bf16[256,256]{1,0:T(8,128)(2,1)S(1)} %fusion.2.refs_0_._), channel_id=1, source_target_pairs={{0,128},{1,129},{2,130},{3,131},{4,132},{5,133},{6,134},{7,135},{8... | collective-permute-start | bytes 393224 | tf_op jit(solution)/shard_map/ppermute | solution.py:271
  19.7 1.3 %collective-permute-start.5 = (bf16[256,256]{1,0:T(8,128)(2,1)S(1)}, bf16[256,256]{1,0:T(8,128)(2,1)S(1)}, u32[]{:S(2)}, u32[]{:S(2)}) collective-permute-start(bf16[256,256]{1,0:T(8,128)(2,1)S(1)} %fusion.2.refs_0_._), channel_id=1, source_target_pairs={{0,192},{1,193},{2,194},{3,195},{4,196},{5,197},{6,198},{7,199},{8... | collective-permute-start | bytes 393224 | tf_op jit(solution)/shard_map/ppermute | solution.py:271
  21.0 0.0 copy-done.3
  21.0 0.8 %row_message.1 = bf16[16,4,24,128]{3,2,1,0:T(8,128)(2,1)} custom-call(s32[1]{0:T(128)S(6)} %copy.9.offset_ref, bf16[1,8192]{1,0:T(2,128)(2,1)S(1)} %copy-done.3, bf16[256,256]{1,0:T(8,128)(2,1)S(1)} %fusion.2.refs_0_._), custom_call_target="tpu_custom_call" | custom-call | flops 49999998976 | bytes 1048576 | tf_op jit(solution)/shard_map/row_message/pallas_call | solution.py:241
  21.8 5.5 %all-to-all-start = ((bf16[64,24,128]{2,1,0:T(8,128)(2,1)}), bf16[64,24,128]{2,1,0:T(8,128)(2,1)S(1)}, u32[]{:S(2)}, u32[]{:S(2)}) async-start(bf16[64,24,128]{2,1,0:T(8,128)(2,1)} %bitcast.2), calls=%async_computation | async-start | bytes 786432 | tf_op jit(solution)/shard_map/all_to_all | solution.py:307
  27.3 0.0 collective-permute-done.3.refs_1_
  27.3 1.8 %collective-permute-start.11 = (bf16[1040,256]{1,0:T(8,128)(2,1)}, bf16[1040,256]{1,0:T(8,128)(2,1)S(1)}, u32[]{:S(2)}, u32[]{:S(2)}) collective-permute-start(bf16[1040,256]{1,0:T(8,128)(2,1)} %pad_maximum_fusion), channel_id=1, source_target_pairs={{0,8},{4,12},{8,0},{12,4},{1,9},{5,13},{9,1},{13,5},{2,10},{6,14},... | collective-permute-start | bytes 1597448 | tf_op jit(solution)/shard_map/ppermute | solution.py:259
  29.1 0.0 collective-permute-done.4.refs_2_
  29.1 0.0 collective-permute-done.5.refs_3_
  29.1 0.0 collective-permute-done.6.refs_4_.m1
  29.1 0.0 collective-permute-done.7.refs_5_.m2
  29.2 5.8 %collective-permute-start.10 = (bf16[256,256]{1,0:T(8,128)(2,1)S(1)}, bf16[256,256]{1,0:T(8,128)(2,1)S(1)}, u32[]{:S(2)}, u32[]{:S(2)}) collective-permute-start(bf16[256,256]{1,0:T(8,128)(2,1)S(1)} %join.2.rest_0_.refs_0_), channel_id=1, source_target_pairs={{0,48},{64,112},{128,176},{192,240},{1,49},{65,113},{129,177},{193... | collective-permute-start | bytes 393224 | tf_op jit(solution)/shard_map/ppermute | solution.py:275
  35.0 1.3 %collective-permute-start.8 = (bf16[256,256]{1,0:T(8,128)(2,1)S(1)}, bf16[256,256]{1,0:T(8,128)(2,1)S(1)}, u32[]{:S(2)}, u32[]{:S(2)}) collective-permute-start(bf16[256,256]{1,0:T(8,128)(2,1)S(1)} %join.2.rest_0_.refs_0_), channel_id=1, source_target_pairs={{0,16},{64,80},{128,144},{192,208},{1,17},{65,81},{129,145},{193,2... | collective-permute-start | bytes 393224 | tf_op jit(solution)/shard_map/ppermute | solution.py:275
  36.3 1.3 %collective-permute-start.9 = (bf16[256,256]{1,0:T(8,128)(2,1)S(1)}, bf16[256,256]{1,0:T(8,128)(2,1)S(1)}, u32[]{:S(2)}, u32[]{:S(2)}) collective-permute-start(bf16[256,256]{1,0:T(8,128)(2,1)S(1)} %join.2.rest_0_.refs_0_), channel_id=1, source_target_pairs={{0,32},{64,96},{128,160},{192,224},{1,33},{65,97},{129,161},{193,2... | collective-permute-start | bytes 393224 | tf_op jit(solution)/shard_map/ppermute | solution.py:275
  37.6 4.6 %collective-permute-done.11.m3 = bf16[1040,256]{1,0:T(8,128)(2,1)S(1)} collective-permute-done((bf16[1040,256]{1,0:T(8,128)(2,1)}, bf16[1040,256]{1,0:T(8,128)(2,1)S(1)}, u32[]{:S(2)}, u32[]{:S(2)}) %collective-permute-start.11) | collective-permute-done | bytes 532512 | tf_op jit(solution)/shard_map/ppermute | solution.py:259
  42.2 0.6 all-to-all-done.msg_ref
  42.8 5.1 %rows_attention.1.refs_4_ = bf16[64,24,128]{2,1,0:T(8,128)(2,1)} custom-call(s32[1]{0:T(128)S(6)} %copy.8.valid_ref, bf16[64,24,128]{2,1,0:T(8,128)(2,1)S(1)} %all-to-all-done.msg_ref, bf16[512,256]{1,0:T(8,128)(2,1)S(1)} %copy-done, bf16[512,256]{1,0:T(8,128)(2,1)S(1)} %copy-done.1, bf16[1040,256]{1,0:T(8,128)(2,1)S(1)} %collective-permute-done.6.refs_4_.m1, ...), custom_call_target="tpu_custom_call" | custom-call | flops 7000000000 | bytes 3145728 | tf_op jit(solution)/shard_map/rows_attention/pallas_call | solution.py:171
  47.9 10.9 %all-to-all-start.1 = ((bf16[64,24,128]{2,1,0:T(8,128)(2,1)}), bf16[64,24,128]{2,1,0:T(8,128)(2,1)S(1)}, u32[]{:S(2)}, u32[]{:S(2)}) async-start(bf16[64,24,128]{2,1,0:T(8,128)(2,1)} %rows_attention.1.refs_4_), calls=%async_computation.1 | async-start | bytes 786432 | tf_op jit(solution)/shard_map/all_to_all | solution.py:312
  58.9 0.0 copy-start.2
  58.9 0.0 collective-permute-done.10.refs_3_
  58.9 0.0 collective-permute-done.8.refs_1_
  58.9 0.0 collective-permute-done.9.refs_2_
  58.9 0.2 collective-permute-start.12
  59.1 2.6 %collective-permute-start.13 = (bf16[256,256]{1,0:T(8,128)(2,1)S(1)}, bf16[256,256]{1,0:T(8,128)(2,1)S(1)}, u32[]{:S(2)}, u32[]{:S(2)}) collective-permute-start(bf16[256,256]{1,0:T(8,128)(2,1)S(1)} %join.3.a0), channel_id=1, source_target_pairs={{0,12},{4,0},{8,4},{12,8},{1,13},{5,1},{9,5},{13,9},{2,14},{6,2},{... | collective-permute-start | bytes 393224 | tf_op jit(solution)/shard_map/ppermute | solution.py:259
  61.7 0.5 collective-permute-start.14
  62.2 2.7 %collective-permute-done.12.a1 = bf16[256,256]{1,0:T(8,128)(2,1)S(1)} collective-permute-done((bf16[256,256]{1,0:T(8,128)(2,1)S(1)}, bf16[256,256]{1,0:T(8,128)(2,1)S(1)}, u32[]{:S(2)}, u32[]{:S(2)}) %collective-permute-start.12) | collective-permute-done | bytes 131104 | tf_op jit(solution)/shard_map/ppermute | solution.py:259
  64.8 1.9 %collective-permute-done.13.a2 = bf16[256,256]{1,0:T(8,128)(2,1)S(1)} collective-permute-done((bf16[256,256]{1,0:T(8,128)(2,1)S(1)}, bf16[256,256]{1,0:T(8,128)(2,1)S(1)}, u32[]{:S(2)}, u32[]{:S(2)}) %collective-permute-start.13) | collective-permute-done | bytes 131104 | tf_op jit(solution)/shard_map/ppermute | solution.py:259
  66.8 0.6 collective-permute-done.14.a3
  67.3 9.9 %block_attention.1 = bf16[512,2048]{1,0:T(8,128)(2,1)} custom-call(s32[1]{0:T(128)S(6)} %copy.8.valid_ref, bf16[512,2048]{1,0:T(8,128)(2,1)S(1)} %copy-done.2, bf16[512,256]{1,0:T(8,128)(2,1)S(1)} %copy-done, bf16[512,256]{1,0:T(8,128)(2,1)S(1)} %copy-done.1, bf16[256,256]{1,0:T(8,128)(2,1)S(1)} %join.3.a0, bf16[256,256]{1,0:T(8,128)(2,1)S(1)} %collective-permute-done.12.a1, ...), custom_call_target="tpu_custom_call" | custom-call | flops 1000000000 | bytes 5242880 | tf_op jit(solution)/shard_map/block_attention/pallas_call | solution.py:93
  77.2 0.0 all-to-all-done.1.msg_ref
  77.2 1.2 %merge.1 = bf16[1,8192]{1,0:T(2,128)(2,1)} custom-call(bf16[64,24,128]{2,1,0:T(8,128)(2,1)S(1)} %all-to-all-done.1.msg_ref), custom_call_target="tpu_custom_call" | custom-call | tf_op jit(solution)/shard_map/merge/pallas_call | solution.py:205
  (10 shorter events, 0.1 us)
Async XLA Ops:
  0.6 9.7 %copy-start = (bf16[512,256]{1,0:T(8,128)(2,1)S(1)}, bf16[512,256]{1,0:T(8,128)(2,1)}, u32[]{:S(2)}) copy-start(bf16[512,256]{1,0:T(8,128)(2,1)} %k_ref.3) | copy-start | bytes 786436
  0.6 9.7 %copy-start.1 = (bf16[512,256]{1,0:T(8,128)(2,1)S(1)}, bf16[512,256]{1,0:T(8,128)(2,1)}, u32[]{:S(2)}) copy-start(bf16[512,256]{1,0:T(8,128)(2,1)} %v_ref.3) | copy-start | bytes 786436
  1.8 13.0 %collective-permute-start = (bf16[256,256]{1,0:T(8,128)(2,1)S(1)}, bf16[256,256]{1,0:T(8,128)(2,1)S(1)}, u32[]{:S(2)}, u32[]{:S(2)}) collective-permute-start(bf16[256,256]{1,0:T(8,128)(2,1)S(1)} %pad_maximum_fusion.1), channel_id=1, source_target_pairs={{0,4},{1,5},{2,6},{3,7}} | collective-permute-start | bytes 393224 | tf_op jit(solution)/shard_map/ppermute | solution.py:266
  5.9 15.1 %copy-start.3 = (bf16[1,8192]{1,0:T(2,128)(2,1)S(1)}, bf16[1,8192]{1,0:T(2,128)(2,1)}, u32[]{:S(2)}) copy-start(bf16[1,8192]{1,0:T(2,128)(2,1)} %q_ref.2) | copy-start | bytes 49156
  5.9 8.9 %collective-permute-start.1 = (bf16[256,256]{1,0:T(8,128)(2,1)S(1)}, bf16[256,256]{1,0:T(8,128)(2,1)S(1)}, u32[]{:S(2)}, u32[]{:S(2)}) collective-permute-start(bf16[256,256]{1,0:T(8,128)(2,1)S(1)} %pad_maximum_fusion.2), channel_id=1, source_target_pairs={{0,8},{1,9},{2,10},{3,11}} | collective-permute-start | bytes 393224 | tf_op jit(solution)/shard_map/ppermute | solution.py:266
  8.2 6.6 %collective-permute-start.2 = (bf16[256,256]{1,0:T(8,128)(2,1)S(1)}, bf16[256,256]{1,0:T(8,128)(2,1)S(1)}, u32[]{:S(2)}, u32[]{:S(2)}) collective-permute-start(bf16[256,256]{1,0:T(8,128)(2,1)S(1)} %pad_maximum_fusion.3), channel_id=1, source_target_pairs={{0,12},{1,13},{2,14},{3,15}} | collective-permute-start | bytes 393224 | tf_op jit(solution)/shard_map/ppermute | solution.py:266
  11.5 17.7 %collective-permute-start.6 = (bf16[1040,256]{1,0:T(8,128)(2,1)}, bf16[1040,256]{1,0:T(8,128)(2,1)S(1)}, u32[]{:S(2)}, u32[]{:S(2)}) collective-permute-start(bf16[1040,256]{1,0:T(8,128)(2,1)} %pad_maximum_fusion), channel_id=1, source_target_pairs={{0,4},{4,8},{8,12},{12,0},{1,5},{5,9},{9,13},{13,1},{2,6},{6,10},{... | collective-permute-start | bytes 1597448 | tf_op jit(solution)/shard_map/ppermute | solution.py:259
  11.5 17.7 %collective-permute-start.7 = (bf16[1040,256]{1,0:T(8,128)(2,1)}, bf16[1040,256]{1,0:T(8,128)(2,1)S(1)}, u32[]{:S(2)}, u32[]{:S(2)}) collective-permute-start(bf16[1040,256]{1,0:T(8,128)(2,1)} %pad_maximum_fusion), channel_id=1, source_target_pairs={{0,12},{4,0},{8,4},{12,8},{1,13},{5,1},{9,5},{13,9},{2,14},{6,2},{... | collective-permute-start | bytes 1597448 | tf_op jit(solution)/shard_map/ppermute | solution.py:259
  14.9 12.4 %collective-permute-start.3 = (bf16[256,256]{1,0:T(8,128)(2,1)S(1)}, bf16[256,256]{1,0:T(8,128)(2,1)S(1)}, u32[]{:S(2)}, u32[]{:S(2)}) collective-permute-start(bf16[256,256]{1,0:T(8,128)(2,1)S(1)} %fusion.2.refs_0_._), channel_id=1, source_target_pairs={{0,64},{1,65},{2,66},{3,67},{4,68},{5,69},{6,70},{7,71},{8,72},{9,... | collective-permute-start | bytes 393224 | tf_op jit(solution)/shard_map/ppermute | solution.py:271
  16.2 12.9 %collective-permute-start.4 = (bf16[256,256]{1,0:T(8,128)(2,1)S(1)}, bf16[256,256]{1,0:T(8,128)(2,1)S(1)}, u32[]{:S(2)}, u32[]{:S(2)}) collective-permute-start(bf16[256,256]{1,0:T(8,128)(2,1)S(1)} %fusion.2.refs_0_._), channel_id=1, source_target_pairs={{0,128},{1,129},{2,130},{3,131},{4,132},{5,133},{6,134},{7,135},{8... | collective-permute-start | bytes 393224 | tf_op jit(solution)/shard_map/ppermute | solution.py:271
  19.7 9.4 %collective-permute-start.5 = (bf16[256,256]{1,0:T(8,128)(2,1)S(1)}, bf16[256,256]{1,0:T(8,128)(2,1)S(1)}, u32[]{:S(2)}, u32[]{:S(2)}) collective-permute-start(bf16[256,256]{1,0:T(8,128)(2,1)S(1)} %fusion.2.refs_0_._), channel_id=1, source_target_pairs={{0,192},{1,193},{2,194},{3,195},{4,196},{5,197},{6,198},{7,199},{8... | collective-permute-start | bytes 393224 | tf_op jit(solution)/shard_map/ppermute | solution.py:271
  21.8 21.0 %all-to-all-start = ((bf16[64,24,128]{2,1,0:T(8,128)(2,1)}), bf16[64,24,128]{2,1,0:T(8,128)(2,1)S(1)}, u32[]{:S(2)}, u32[]{:S(2)}) async-start(bf16[64,24,128]{2,1,0:T(8,128)(2,1)} %bitcast.2), calls=%async_computation | async-start | bytes 786432 | tf_op jit(solution)/shard_map/all_to_all | solution.py:307
  27.3 14.9 %collective-permute-start.11 = (bf16[1040,256]{1,0:T(8,128)(2,1)}, bf16[1040,256]{1,0:T(8,128)(2,1)S(1)}, u32[]{:S(2)}, u32[]{:S(2)}) collective-permute-start(bf16[1040,256]{1,0:T(8,128)(2,1)} %pad_maximum_fusion), channel_id=1, source_target_pairs={{0,8},{4,12},{8,0},{12,4},{1,9},{5,13},{9,1},{13,5},{2,10},{6,14},... | collective-permute-start | bytes 1597448 | tf_op jit(solution)/shard_map/ppermute | solution.py:259
  29.2 29.7 %collective-permute-start.10 = (bf16[256,256]{1,0:T(8,128)(2,1)S(1)}, bf16[256,256]{1,0:T(8,128)(2,1)S(1)}, u32[]{:S(2)}, u32[]{:S(2)}) collective-permute-start(bf16[256,256]{1,0:T(8,128)(2,1)S(1)} %join.2.rest_0_.refs_0_), channel_id=1, source_target_pairs={{0,48},{64,112},{128,176},{192,240},{1,49},{65,113},{129,177},{193... | collective-permute-start | bytes 393224 | tf_op jit(solution)/shard_map/ppermute | solution.py:275
  35.0 23.9 %collective-permute-start.8 = (bf16[256,256]{1,0:T(8,128)(2,1)S(1)}, bf16[256,256]{1,0:T(8,128)(2,1)S(1)}, u32[]{:S(2)}, u32[]{:S(2)}) collective-permute-start(bf16[256,256]{1,0:T(8,128)(2,1)S(1)} %join.2.rest_0_.refs_0_), channel_id=1, source_target_pairs={{0,16},{64,80},{128,144},{192,208},{1,17},{65,81},{129,145},{193,2... | collective-permute-start | bytes 393224 | tf_op jit(solution)/shard_map/ppermute | solution.py:275
  36.3 22.6 %collective-permute-start.9 = (bf16[256,256]{1,0:T(8,128)(2,1)S(1)}, bf16[256,256]{1,0:T(8,128)(2,1)S(1)}, u32[]{:S(2)}, u32[]{:S(2)}) collective-permute-start(bf16[256,256]{1,0:T(8,128)(2,1)S(1)} %join.2.rest_0_.refs_0_), channel_id=1, source_target_pairs={{0,32},{64,96},{128,160},{192,224},{1,33},{65,97},{129,161},{193,2... | collective-permute-start | bytes 393224 | tf_op jit(solution)/shard_map/ppermute | solution.py:275
  47.9 29.3 %all-to-all-start.1 = ((bf16[64,24,128]{2,1,0:T(8,128)(2,1)}), bf16[64,24,128]{2,1,0:T(8,128)(2,1)S(1)}, u32[]{:S(2)}, u32[]{:S(2)}) async-start(bf16[64,24,128]{2,1,0:T(8,128)(2,1)} %rows_attention.1.refs_4_), calls=%async_computation.1 | async-start | bytes 786432 | tf_op jit(solution)/shard_map/all_to_all | solution.py:312
  58.9 8.5 %copy-start.2 = (bf16[512,2048]{1,0:T(8,128)(2,1)S(1)}, bf16[512,2048]{1,0:T(8,128)(2,1)}, u32[]{:S(2)}) copy-start(bf16[512,2048]{1,0:T(8,128)(2,1)} %q_ref.3) | copy-start | bytes 6291460
  58.9 5.9 %collective-permute-start.12 = (bf16[256,256]{1,0:T(8,128)(2,1)S(1)}, bf16[256,256]{1,0:T(8,128)(2,1)S(1)}, u32[]{:S(2)}, u32[]{:S(2)}) collective-permute-start(bf16[256,256]{1,0:T(8,128)(2,1)S(1)} %join.3.a0), channel_id=1, source_target_pairs={{0,4},{4,8},{8,12},{12,0},{1,5},{5,9},{9,13},{13,1},{2,6},{6,10},{... | collective-permute-start | bytes 393224 | tf_op jit(solution)/shard_map/ppermute | solution.py:259
  59.1 7.7 %collective-permute-start.13 = (bf16[256,256]{1,0:T(8,128)(2,1)S(1)}, bf16[256,256]{1,0:T(8,128)(2,1)S(1)}, u32[]{:S(2)}, u32[]{:S(2)}) collective-permute-start(bf16[256,256]{1,0:T(8,128)(2,1)S(1)} %join.3.a0), channel_id=1, source_target_pairs={{0,12},{4,0},{8,4},{12,8},{1,13},{5,1},{9,5},{13,9},{2,14},{6,2},{... | collective-permute-start | bytes 393224 | tf_op jit(solution)/shard_map/ppermute | solution.py:259
  61.7 5.6 %collective-permute-start.14 = (bf16[256,256]{1,0:T(8,128)(2,1)S(1)}, bf16[256,256]{1,0:T(8,128)(2,1)S(1)}, u32[]{:S(2)}, u32[]{:S(2)}) collective-permute-start(bf16[256,256]{1,0:T(8,128)(2,1)S(1)} %join.3.a0), channel_id=1, source_target_pairs={{0,8},{4,12},{8,0},{12,4},{1,9},{5,13},{9,1},{13,5},{2,10},{6,14},... | collective-permute-start | bytes 393224 | tf_op jit(solution)/shard_map/ppermute | solution.py:259

commit v4 on v3

--- a/solution.py
+++ b/solution.py
@@ -262,13 +262,13 @@
 def anchor_quarters(k, v):
     quarters = [jnp.concatenate([k[r : r + QUARTER], v[r : r + QUARTER]]) for r in range(0, BLK, QUARTER)]
     current = jnp.where(lax.axis_index(CTX) == 0, quarters[0], jnp.zeros_like(quarters[0]))
-    for y in range(1, NY):
+    for y in (1, 3, 2):
         current = current + lax.ppermute(quarters[y], CTX, [(0, y)])
     return current
 
 
 def anchor_tree(current, after):
-    sent = [lax.ppermute(current, ZX, [(0, place(z, 0))]) for z in (2, 4, 6)]
+    sent = [lax.ppermute(current, ZX, [(0, place(z, 0))]) for z in (2, 6, 4)]
     current = join([current] + sent, after)
     even = (0, 2, 4, 6)
     sent = [

time: 79.4 us -> 78.8 us (level)
  no operation moved by 1% of the time
where the time goes in v4:
time: 78.8 us; the launch traced here: 77.8 us
  starting transfers between devices  45.6 us (58%)
  Pallas kernels  17.1 us (22%)
  waiting for transfers between devices  10.4 us (13%)
  between operations  2.23 us (3%)
  local copies, waits for them, and re-layouts  1.27 us (2%)
  other arithmetic  1.26 us (2%)
    all_to_all x1, starting transfers between devices, on_device(): partial = lax.all_to_all(partial, PLANE, 0, 0, tiled=True)  10.9 us
    pallas_call x1, Pallas kernels, block_attention(): pl.pallas_call(functools.partial(block_kernel, heads, chunk, stack), grid...  9.93 us
    ppermute x6, waiting for transfers between devices, to_ring(): return [lax.ppermute(array, 'y', shift(NY, by)) for by in (1, -1, 2)]  9.77 us
    ppermute x3, starting transfers between devices, anchor_tree(): lax.ppermute(current, ZX, [(place(z, 0), place(z + dz, xh)) for z in even])  8.37 us
    ppermute x6, starting transfers between devices, to_ring(): return [lax.ppermute(array, 'y', shift(NY, by)) for by in (1, -1, 2)]  7.71 us
    ppermute x3, starting transfers between devices, anchor_quarters(): current = current + lax.ppermute(quarters[y], CTX, [(0, y)])  7.44 us
    ppermute x3, starting transfers between devices, anchor_tree(): sent = [lax.ppermute(current, ZX, [(0, place(z, 0))]) for z in (2, 6, 4)]  5.61 us
    all_to_all x1, starting transfers between devices, on_device(): message = lax.all_to_all(message, PLANE, 0, 0, tiled=True)  5.51 us
  transfers between devices with their start and end apart: 17, of which 5 were waited for; matrix products, arithmetic and copies ran while one was open for 2% of the time, Pallas kernels for 20%

profile of v4, /device:TPU:1, one launch (start us, length us, event | category | flops | bytes accessed | tf_op | source)
XLA Modules:
  0.0 77.8 jit_solution(13478637845964866045)
XLA Ops:
  0.6 0.0 copy-start
  0.6 0.0 copy-start.1
  0.6 1.2 %fusion.3 = (bf16[128,256]{1,0:T(8,128)(2,1)S(1)}, bf16[128,256]{1,0:T(8,128)(2,1)S(1)}, bf16[128,256]{1,0:T(8,128)(2,1)S(1)}, bf16[128,256]{1,0:T(8,128)(2,1)S(...) fusion(bf16[512,256]{1,0:T(8,128)(2,1)} %k_ref.3, ...), kind=kLoop, calls=%fused_computation.8 | loop fusion | bytes 1048576 | tf_op jit(solution)/shard_map/slice | solution.py:263
  1.8 4.0 %collective-permute-start = (bf16[256,256]{1,0:T(8,128)(2,1)S(1)}, bf16[256,256]{1,0:T(8,128)(2,1)S(1)}, u32[]{:S(2)}, u32[]{:S(2)}) collective-permute-start(bf16[256,256]{1,0:T(8,128)(2,1)S(1)} %pad_maximum_fusion.1), channel_id=1, source_target_pairs={{0,4},{1,5},{2,6},{3,7}} | collective-permute-start | bytes 393224 | tf_op jit(solution)/shard_map/ppermute | solution.py:266
  5.9 0.0 copy-start.3
  5.9 2.1 %collective-permute-start.1 = (bf16[256,256]{1,0:T(8,128)(2,1)S(1)}, bf16[256,256]{1,0:T(8,128)(2,1)S(1)}, u32[]{:S(2)}, u32[]{:S(2)}) collective-permute-start(bf16[256,256]{1,0:T(8,128)(2,1)S(1)} %pad_maximum_fusion.2), channel_id=1, source_target_pairs={{0,12},{1,13},{2,14},{3,15}} | collective-permute-start | bytes 393224 | tf_op jit(solution)/shard_map/ppermute | solution.py:266
  8.0 1.3 %collective-permute-start.2 = (bf16[256,256]{1,0:T(8,128)(2,1)S(1)}, bf16[256,256]{1,0:T(8,128)(2,1)S(1)}, u32[]{:S(2)}, u32[]{:S(2)}) collective-permute-start(bf16[256,256]{1,0:T(8,128)(2,1)S(1)} %pad_maximum_fusion.3), channel_id=1, source_target_pairs={{0,8},{1,9},{2,10},{3,11}} | collective-permute-start | bytes 393224 | tf_op jit(solution)/shard_map/ppermute | solution.py:266
  10.0 0.1 pad.2.clone
  10.1 0.0 copy-done
  10.1 0.0 copy-done.1
  10.1 1.1 %pad_maximum_fusion = bf16[1040,256]{1,0:T(8,128)(2,1)} fusion(bf16[512,256]{1,0:T(8,128)(2,1)S(1)} %copy-done.1, bf16[512,256]{1,0:T(8,128)(2,1)S(1)} %copy-done, bf16[1040]{0:T(1024)(128)(2,1)S(1)} %pad.2.clone, bf16[1040]{0:T(1024)(128)(2,1)S(1)} %pad.1.clone), kind=kLoop, calls=%fused_computation | loop fusion | flops 2129920 | bytes 1060928 | tf_op jit(solution)/shard_map/concatenate | solution.py:303
  11.3 0.0 collective-permute-start.6
  11.3 2.7 %collective-permute-start.7 = (bf16[1040,256]{1,0:T(8,128)(2,1)}, bf16[1040,256]{1,0:T(8,128)(2,1)S(1)}, u32[]{:S(2)}, u32[]{:S(2)}) collective-permute-start(bf16[1040,256]{1,0:T(8,128)(2,1)} %pad_maximum_fusion), channel_id=1, source_target_pairs={{0,12},{4,0},{8,4},{12,8},{1,13},{5,1},{9,5},{13,9},{2,14},{6,2},{... | collective-permute-start | bytes 1597448 | tf_op jit(solution)/shard_map/ppermute | solution.py:259
  14.6 0.0 collective-permute-done
  14.6 0.0 collective-permute-done.1
  14.6 0.0 collective-permute-done.2
  14.6 0.1 fusion.2.refs_0_._
  14.7 1.3 %collective-permute-start.3 = (bf16[256,256]{1,0:T(8,128)(2,1)S(1)}, bf16[256,256]{1,0:T(8,128)(2,1)S(1)}, u32[]{:S(2)}, u32[]{:S(2)}) collective-permute-start(bf16[256,256]{1,0:T(8,128)(2,1)S(1)} %fusion.2.refs_0_._), channel_id=1, source_target_pairs={{0,64},{1,65},{2,66},{3,67},{4,68},{5,69},{6,70},{7,71},{8,72},{9,... | collective-permute-start | bytes 393224 | tf_op jit(solution)/shard_map/ppermute | solution.py:271
  16.0 2.8 %collective-permute-start.4 = (bf16[256,256]{1,0:T(8,128)(2,1)S(1)}, bf16[256,256]{1,0:T(8,128)(2,1)S(1)}, u32[]{:S(2)}, u32[]{:S(2)}) collective-permute-start(bf16[256,256]{1,0:T(8,128)(2,1)S(1)} %fusion.2.refs_0_._), channel_id=1, source_target_pairs={{0,192},{1,193},{2,194},{3,195},{4,196},{5,197},{6,198},{7,199},{8... | collective-permute-start | bytes 393224 | tf_op jit(solution)/shard_map/ppermute | solution.py:271
  18.8 1.6 %collective-permute-start.5 = (bf16[256,256]{1,0:T(8,128)(2,1)S(1)}, bf16[256,256]{1,0:T(8,128)(2,1)S(1)}, u32[]{:S(2)}, u32[]{:S(2)}) collective-permute-start(bf16[256,256]{1,0:T(8,128)(2,1)S(1)} %fusion.2.refs_0_._), channel_id=1, source_target_pairs={{0,128},{1,129},{2,130},{3,131},{4,132},{5,133},{6,134},{7,135},{8... | collective-permute-start | bytes 393224 | tf_op jit(solution)/shard_map/ppermute | solution.py:271
  20.4 0.8 %row_message.1 = bf16[16,4,24,128]{3,2,1,0:T(8,128)(2,1)} custom-call(s32[1]{0:T(128)S(6)} %copy.9.offset_ref, bf16[1,8192]{1,0:T(2,128)(2,1)S(1)} %copy-done.3, bf16[256,256]{1,0:T(8,128)(2,1)S(1)} %fusion.2.refs_0_._), custom_call_target="tpu_custom_call" | custom-call | flops 49999998976 | bytes 1048576 | tf_op jit(solution)/shard_map/row_message/pallas_call | solution.py:241
  21.2 5.5 %all-to-all-start = ((bf16[64,24,128]{2,1,0:T(8,128)(2,1)}), bf16[64,24,128]{2,1,0:T(8,128)(2,1)S(1)}, u32[]{:S(2)}, u32[]{:S(2)}) async-start(bf16[64,24,128]{2,1,0:T(8,128)(2,1)} %bitcast.2), calls=%async_computation | async-start | bytes 786432 | tf_op jit(solution)/shard_map/all_to_all | solution.py:307
  26.7 0.0 collective-permute-done.3.refs_1_
  26.7 1.8 %collective-permute-start.11 = (bf16[1040,256]{1,0:T(8,128)(2,1)}, bf16[1040,256]{1,0:T(8,128)(2,1)S(1)}, u32[]{:S(2)}, u32[]{:S(2)}) collective-permute-start(bf16[1040,256]{1,0:T(8,128)(2,1)} %pad_maximum_fusion), channel_id=1, source_target_pairs={{0,8},{4,12},{8,0},{12,4},{1,9},{5,13},{9,1},{13,5},{2,10},{6,14},... | collective-permute-start | bytes 1597448 | tf_op jit(solution)/shard_map/ppermute | solution.py:259
  28.5 0.0 collective-permute-done.4.refs_2_
  28.5 0.0 collective-permute-done.5.refs_3_
  28.5 0.0 collective-permute-done.6.refs_4_.m1
  28.5 0.0 collective-permute-done.7.refs_5_.m2
  28.6 5.8 %collective-permute-start.10 = (bf16[256,256]{1,0:T(8,128)(2,1)S(1)}, bf16[256,256]{1,0:T(8,128)(2,1)S(1)}, u32[]{:S(2)}, u32[]{:S(2)}) collective-permute-start(bf16[256,256]{1,0:T(8,128)(2,1)S(1)} %join.2.rest_0_.refs_0_), channel_id=1, source_target_pairs={{0,48},{64,112},{128,176},{192,240},{1,49},{65,113},{129,177},{193... | collective-permute-start | bytes 393224 | tf_op jit(solution)/shard_map/ppermute | solution.py:275
  34.4 1.3 %collective-permute-start.8 = (bf16[256,256]{1,0:T(8,128)(2,1)S(1)}, bf16[256,256]{1,0:T(8,128)(2,1)S(1)}, u32[]{:S(2)}, u32[]{:S(2)}) collective-permute-start(bf16[256,256]{1,0:T(8,128)(2,1)S(1)} %join.2.rest_0_.refs_0_), channel_id=1, source_target_pairs={{0,16},{64,80},{128,144},{192,208},{1,17},{65,81},{129,145},{193,2... | collective-permute-start | bytes 393224 | tf_op jit(solution)/shard_map/ppermute | solution.py:275
  35.7 1.3 %collective-permute-start.9 = (bf16[256,256]{1,0:T(8,128)(2,1)S(1)}, bf16[256,256]{1,0:T(8,128)(2,1)S(1)}, u32[]{:S(2)}, u32[]{:S(2)}) collective-permute-start(bf16[256,256]{1,0:T(8,128)(2,1)S(1)} %join.2.rest_0_.refs_0_), channel_id=1, source_target_pairs={{0,32},{64,96},{128,160},{192,224},{1,33},{65,97},{129,161},{193,2... | collective-permute-start | bytes 393224 | tf_op jit(solution)/shard_map/ppermute | solution.py:275
  37.0 4.6 %collective-permute-done.11.m3 = bf16[1040,256]{1,0:T(8,128)(2,1)S(1)} collective-permute-done((bf16[1040,256]{1,0:T(8,128)(2,1)}, bf16[1040,256]{1,0:T(8,128)(2,1)S(1)}, u32[]{:S(2)}, u32[]{:S(2)}) %collective-permute-start.11) | collective-permute-done | bytes 532512 | tf_op jit(solution)/shard_map/ppermute | solution.py:259
  41.6 0.6 all-to-all-done.msg_ref
  42.2 5.1 %rows_attention.1.refs_4_ = bf16[64,24,128]{2,1,0:T(8,128)(2,1)} custom-call(s32[1]{0:T(128)S(6)} %copy.8.valid_ref, bf16[64,24,128]{2,1,0:T(8,128)(2,1)S(1)} %all-to-all-done.msg_ref, bf16[512,256]{1,0:T(8,128)(2,1)S(1)} %copy-done, bf16[512,256]{1,0:T(8,128)(2,1)S(1)} %copy-done.1, bf16[1040,256]{1,0:T(8,128)(2,1)S(1)} %collective-permute-done.6.refs_4_.m1, ...), custom_call_target="tpu_custom_call" | custom-call | flops 7000000000 | bytes 3145728 | tf_op jit(solution)/shard_map/rows_attention/pallas_call | solution.py:171
  47.3 10.9 %all-to-all-start.1 = ((bf16[64,24,128]{2,1,0:T(8,128)(2,1)}), bf16[64,24,128]{2,1,0:T(8,128)(2,1)S(1)}, u32[]{:S(2)}, u32[]{:S(2)}) async-start(bf16[64,24,128]{2,1,0:T(8,128)(2,1)} %rows_attention.1.refs_4_), calls=%async_computation.1 | async-start | bytes 786432 | tf_op jit(solution)/shard_map/all_to_all | solution.py:312
  58.2 0.0 copy-start.2
  58.2 0.0 collective-permute-done.10.refs_3_
  58.2 0.0 collective-permute-done.8.refs_1_
  58.3 0.0 collective-permute-done.9.refs_2_
  58.3 0.2 collective-permute-start.12
  58.5 2.6 %collective-permute-start.13 = (bf16[256,256]{1,0:T(8,128)(2,1)S(1)}, bf16[256,256]{1,0:T(8,128)(2,1)S(1)}, u32[]{:S(2)}, u32[]{:S(2)}) collective-permute-start(bf16[256,256]{1,0:T(8,128)(2,1)S(1)} %join.3.a0), channel_id=1, source_target_pairs={{0,12},{4,0},{8,4},{12,8},{1,13},{5,1},{9,5},{13,9},{2,14},{6,2},{... | collective-permute-start | bytes 393224 | tf_op jit(solution)/shard_map/ppermute | solution.py:259
  61.1 0.5 collective-permute-start.14
  61.6 2.7 %collective-permute-done.12.a1 = bf16[256,256]{1,0:T(8,128)(2,1)S(1)} collective-permute-done((bf16[256,256]{1,0:T(8,128)(2,1)S(1)}, bf16[256,256]{1,0:T(8,128)(2,1)S(1)}, u32[]{:S(2)}, u32[]{:S(2)}) %collective-permute-start.12) | collective-permute-done | bytes 131104 | tf_op jit(solution)/shard_map/ppermute | solution.py:259
  64.2 1.9 %collective-permute-done.13.a2 = bf16[256,256]{1,0:T(8,128)(2,1)S(1)} collective-permute-done((bf16[256,256]{1,0:T(8,128)(2,1)S(1)}, bf16[256,256]{1,0:T(8,128)(2,1)S(1)}, u32[]{:S(2)}, u32[]{:S(2)}) %collective-permute-start.13) | collective-permute-done | bytes 131104 | tf_op jit(solution)/shard_map/ppermute | solution.py:259
  66.1 0.6 collective-permute-done.14.a3
  66.7 9.9 %block_attention.1 = bf16[512,2048]{1,0:T(8,128)(2,1)} custom-call(s32[1]{0:T(128)S(6)} %copy.8.valid_ref, bf16[512,2048]{1,0:T(8,128)(2,1)S(1)} %copy-done.2, bf16[512,256]{1,0:T(8,128)(2,1)S(1)} %copy-done, bf16[512,256]{1,0:T(8,128)(2,1)S(1)} %copy-done.1, bf16[256,256]{1,0:T(8,128)(2,1)S(1)} %join.3.a0, bf16[256,256]{1,0:T(8,128)(2,1)S(1)} %collective-permute-done.12.a1, ...), custom_call_target="tpu_custom_call" | custom-call | flops 1000000000 | bytes 5242880 | tf_op jit(solution)/shard_map/block_attention/pallas_call | solution.py:93
  76.6 0.0 all-to-all-done.1.msg_ref
  76.6 1.2 %merge.1 = bf16[1,8192]{1,0:T(2,128)(2,1)} custom-call(bf16[64,24,128]{2,1,0:T(8,128)(2,1)S(1)} %all-to-all-done.1.msg_ref), custom_call_target="tpu_custom_call" | custom-call | tf_op jit(solution)/shard_map/merge/pallas_call | solution.py:205
  (10 shorter events, 0.1 us)
Async XLA Ops:
  0.6 9.5 %copy-start = (bf16[512,256]{1,0:T(8,128)(2,1)S(1)}, bf16[512,256]{1,0:T(8,128)(2,1)}, u32[]{:S(2)}) copy-start(bf16[512,256]{1,0:T(8,128)(2,1)} %k_ref.3) | copy-start | bytes 786436
  0.6 9.5 %copy-start.1 = (bf16[512,256]{1,0:T(8,128)(2,1)S(1)}, bf16[512,256]{1,0:T(8,128)(2,1)}, u32[]{:S(2)}) copy-start(bf16[512,256]{1,0:T(8,128)(2,1)} %v_ref.3) | copy-start | bytes 786436
  1.8 12.8 %collective-permute-start = (bf16[256,256]{1,0:T(8,128)(2,1)S(1)}, bf16[256,256]{1,0:T(8,128)(2,1)S(1)}, u32[]{:S(2)}, u32[]{:S(2)}) collective-permute-start(bf16[256,256]{1,0:T(8,128)(2,1)S(1)} %pad_maximum_fusion.1), channel_id=1, source_target_pairs={{0,4},{1,5},{2,6},{3,7}} | collective-permute-start | bytes 393224 | tf_op jit(solution)/shard_map/ppermute | solution.py:266
  5.9 14.5 %copy-start.3 = (bf16[1,8192]{1,0:T(2,128)(2,1)S(1)}, bf16[1,8192]{1,0:T(2,128)(2,1)}, u32[]{:S(2)}) copy-start(bf16[1,8192]{1,0:T(2,128)(2,1)} %q_ref.2) | copy-start | bytes 49156
  5.9 8.7 %collective-permute-start.1 = (bf16[256,256]{1,0:T(8,128)(2,1)S(1)}, bf16[256,256]{1,0:T(8,128)(2,1)S(1)}, u32[]{:S(2)}, u32[]{:S(2)}) collective-permute-start(bf16[256,256]{1,0:T(8,128)(2,1)S(1)} %pad_maximum_fusion.2), channel_id=1, source_target_pairs={{0,12},{1,13},{2,14},{3,15}} | collective-permute-start | bytes 393224 | tf_op jit(solution)/shard_map/ppermute | solution.py:266
  8.0 6.6 %collective-permute-start.2 = (bf16[256,256]{1,0:T(8,128)(2,1)S(1)}, bf16[256,256]{1,0:T(8,128)(2,1)S(1)}, u32[]{:S(2)}, u32[]{:S(2)}) collective-permute-start(bf16[256,256]{1,0:T(8,128)(2,1)S(1)} %pad_maximum_fusion.3), channel_id=1, source_target_pairs={{0,8},{1,9},{2,10},{3,11}} | collective-permute-start | bytes 393224 | tf_op jit(solution)/shard_map/ppermute | solution.py:266
  11.3 17.2 %collective-permute-start.6 = (bf16[1040,256]{1,0:T(8,128)(2,1)}, bf16[1040,256]{1,0:T(8,128)(2,1)S(1)}, u32[]{:S(2)}, u32[]{:S(2)}) collective-permute-start(bf16[1040,256]{1,0:T(8,128)(2,1)} %pad_maximum_fusion), channel_id=1, source_target_pairs={{0,4},{4,8},{8,12},{12,0},{1,5},{5,9},{9,13},{13,1},{2,6},{6,10},{... | collective-permute-start | bytes 1597448 | tf_op jit(solution)/shard_map/ppermute | solution.py:259
  11.3 17.2 %collective-permute-start.7 = (bf16[1040,256]{1,0:T(8,128)(2,1)}, bf16[1040,256]{1,0:T(8,128)(2,1)S(1)}, u32[]{:S(2)}, u32[]{:S(2)}) collective-permute-start(bf16[1040,256]{1,0:T(8,128)(2,1)} %pad_maximum_fusion), channel_id=1, source_target_pairs={{0,12},{4,0},{8,4},{12,8},{1,13},{5,1},{9,5},{13,9},{2,14},{6,2},{... | collective-permute-start | bytes 1597448 | tf_op jit(solution)/shard_map/ppermute | solution.py:259
  14.7 12.0 %collective-permute-start.3 = (bf16[256,256]{1,0:T(8,128)(2,1)S(1)}, bf16[256,256]{1,0:T(8,128)(2,1)S(1)}, u32[]{:S(2)}, u32[]{:S(2)}) collective-permute-start(bf16[256,256]{1,0:T(8,128)(2,1)S(1)} %fusion.2.refs_0_._), channel_id=1, source_target_pairs={{0,64},{1,65},{2,66},{3,67},{4,68},{5,69},{6,70},{7,71},{8,72},{9,... | collective-permute-start | bytes 393224 | tf_op jit(solution)/shard_map/ppermute | solution.py:271
  16.0 12.5 %collective-permute-start.4 = (bf16[256,256]{1,0:T(8,128)(2,1)S(1)}, bf16[256,256]{1,0:T(8,128)(2,1)S(1)}, u32[]{:S(2)}, u32[]{:S(2)}) collective-permute-start(bf16[256,256]{1,0:T(8,128)(2,1)S(1)} %fusion.2.refs_0_._), channel_id=1, source_target_pairs={{0,192},{1,193},{2,194},{3,195},{4,196},{5,197},{6,198},{7,199},{8... | collective-permute-start | bytes 393224 | tf_op jit(solution)/shard_map/ppermute | solution.py:271
  18.8 9.7 %collective-permute-start.5 = (bf16[256,256]{1,0:T(8,128)(2,1)S(1)}, bf16[256,256]{1,0:T(8,128)(2,1)S(1)}, u32[]{:S(2)}, u32[]{:S(2)}) collective-permute-start(bf16[256,256]{1,0:T(8,128)(2,1)S(1)} %fusion.2.refs_0_._), channel_id=1, source_target_pairs={{0,128},{1,129},{2,130},{3,131},{4,132},{5,133},{6,134},{7,135},{8... | collective-permute-start | bytes 393224 | tf_op jit(solution)/shard_map/ppermute | solution.py:271
  21.2 21.0 %all-to-all-start = ((bf16[64,24,128]{2,1,0:T(8,128)(2,1)}), bf16[64,24,128]{2,1,0:T(8,128)(2,1)S(1)}, u32[]{:S(2)}, u32[]{:S(2)}) async-start(bf16[64,24,128]{2,1,0:T(8,128)(2,1)} %bitcast.2), calls=%async_computation | async-start | bytes 786432 | tf_op jit(solution)/shard_map/all_to_all | solution.py:307
  26.7 14.9 %collective-permute-start.11 = (bf16[1040,256]{1,0:T(8,128)(2,1)}, bf16[1040,256]{1,0:T(8,128)(2,1)S(1)}, u32[]{:S(2)}, u32[]{:S(2)}) collective-permute-start(bf16[1040,256]{1,0:T(8,128)(2,1)} %pad_maximum_fusion), channel_id=1, source_target_pairs={{0,8},{4,12},{8,0},{12,4},{1,9},{5,13},{9,1},{13,5},{2,10},{6,14},... | collective-permute-start | bytes 1597448 | tf_op jit(solution)/shard_map/ppermute | solution.py:259
  28.6 29.7 %collective-permute-start.10 = (bf16[256,256]{1,0:T(8,128)(2,1)S(1)}, bf16[256,256]{1,0:T(8,128)(2,1)S(1)}, u32[]{:S(2)}, u32[]{:S(2)}) collective-permute-start(bf16[256,256]{1,0:T(8,128)(2,1)S(1)} %join.2.rest_0_.refs_0_), channel_id=1, source_target_pairs={{0,48},{64,112},{128,176},{192,240},{1,49},{65,113},{129,177},{193... | collective-permute-start | bytes 393224 | tf_op jit(solution)/shard_map/ppermute | solution.py:275
  34.4 23.9 %collective-permute-start.8 = (bf16[256,256]{1,0:T(8,128)(2,1)S(1)}, bf16[256,256]{1,0:T(8,128)(2,1)S(1)}, u32[]{:S(2)}, u32[]{:S(2)}) collective-permute-start(bf16[256,256]{1,0:T(8,128)(2,1)S(1)} %join.2.rest_0_.refs_0_), channel_id=1, source_target_pairs={{0,16},{64,80},{128,144},{192,208},{1,17},{65,81},{129,145},{193,2... | collective-permute-start | bytes 393224 | tf_op jit(solution)/shard_map/ppermute | solution.py:275
  35.7 22.6 %collective-permute-start.9 = (bf16[256,256]{1,0:T(8,128)(2,1)S(1)}, bf16[256,256]{1,0:T(8,128)(2,1)S(1)}, u32[]{:S(2)}, u32[]{:S(2)}) collective-permute-start(bf16[256,256]{1,0:T(8,128)(2,1)S(1)} %join.2.rest_0_.refs_0_), channel_id=1, source_target_pairs={{0,32},{64,96},{128,160},{192,224},{1,33},{65,97},{129,161},{193,2... | collective-permute-start | bytes 393224 | tf_op jit(solution)/shard_map/ppermute | solution.py:275
  47.3 29.3 %all-to-all-start.1 = ((bf16[64,24,128]{2,1,0:T(8,128)(2,1)}), bf16[64,24,128]{2,1,0:T(8,128)(2,1)S(1)}, u32[]{:S(2)}, u32[]{:S(2)}) async-start(bf16[64,24,128]{2,1,0:T(8,128)(2,1)} %rows_attention.1.refs_4_), calls=%async_computation.1 | async-start | bytes 786432 | tf_op jit(solution)/shard_map/all_to_all | solution.py:312
  58.2 8.5 %copy-start.2 = (bf16[512,2048]{1,0:T(8,128)(2,1)S(1)}, bf16[512,2048]{1,0:T(8,128)(2,1)}, u32[]{:S(2)}) copy-start(bf16[512,2048]{1,0:T(8,128)(2,1)} %q_ref.3) | copy-start | bytes 6291460
  58.3 5.9 %collective-permute-start.12 = (bf16[256,256]{1,0:T(8,128)(2,1)S(1)}, bf16[256,256]{1,0:T(8,128)(2,1)S(1)}, u32[]{:S(2)}, u32[]{:S(2)}) collective-permute-start(bf16[256,256]{1,0:T(8,128)(2,1)S(1)} %join.3.a0), channel_id=1, source_target_pairs={{0,4},{4,8},{8,12},{12,0},{1,5},{5,9},{9,13},{13,1},{2,6},{6,10},{... | collective-permute-start | bytes 393224 | tf_op jit(solution)/shard_map/ppermute | solution.py:259
  58.5 7.7 %collective-permute-start.13 = (bf16[256,256]{1,0:T(8,128)(2,1)S(1)}, bf16[256,256]{1,0:T(8,128)(2,1)S(1)}, u32[]{:S(2)}, u32[]{:S(2)}) collective-permute-start(bf16[256,256]{1,0:T(8,128)(2,1)S(1)} %join.3.a0), channel_id=1, source_target_pairs={{0,12},{4,0},{8,4},{12,8},{1,13},{5,1},{9,5},{13,9},{2,14},{6,2},{... | collective-permute-start | bytes 393224 | tf_op jit(solution)/shard_map/ppermute | solution.py:259
  61.1 5.6 %collective-permute-start.14 = (bf16[256,256]{1,0:T(8,128)(2,1)S(1)}, bf16[256,256]{1,0:T(8,128)(2,1)S(1)}, u32[]{:S(2)}, u32[]{:S(2)}) collective-permute-start(bf16[256,256]{1,0:T(8,128)(2,1)S(1)} %join.3.a0), channel_id=1, source_target_pairs={{0,8},{4,12},{8,0},{12,4},{1,9},{5,13},{9,1},{13,5},{2,10},{6,14},... | collective-permute-start | bytes 393224 | tf_op jit(solution)/shard_map/ppermute | solution.py:259
